TPU v7x, 512 devices: a whole 4x8x8 slice. The times are simulated.
512 devices in a mesh: node: 128 (over y, z_hi, x), slab: 4 (over z_lo, core).
Axes of the slice: x: 4, y: 8, z: 8 (z_hi: 4, z_lo: 2; z = z_hi * 2 + z_lo), core: 2. Of those that a mesh axis runs over, the one named last changes fastest.
Arguments:
- points: float32 [65536, 64], P(('node', 'slab')), may hold values from -6 to 6
- probes: float32 [65536, 128], P(('node', 'slab')), may hold values from -1.5 to 1.5
- leaf: int32 [65536, 1], P(('node', 'slab')), may hold values from 0 to 127; in each aligned block of 128 rows (0 to 127, 128 to 255, ...) at most 4 rows name the same one
Outputs:
- sketches: float32 [65536, 128], P(('node', 'slab'))
Inputs may be any that keep to these rules, and one draw needn't show every extreme that they name: `leaf`: among the 128 points of one device, at most 4 name any one cluster, and exactly 4 name some cluster on some device.
All inputs are finite; a program needn't handle non-finite values.
Results may differ from a plain program's by a relative error of at most 0.00008.
Values sent between devices are 32-bit elements; how exact they have to be, the bound alone decides.
No kernel may reach another device: no remote copies, remote signals or barrier semaphores. Data moves between devices by JAX's collectives and lax.ppermute only.
A program may use at most 64 MiB of HBM per device.

v0:
```python
import jax
import jax.numpy as jnp
from jax import lax
from jax.sharding import PartitionSpec as P

kernel_scale = 1.0 / 64.0


def swapped(value, axis, bit):
    mask = 2**bit
    pairs = [(source, source ^ mask) for source in range(lax.axis_size(axis))]
    return lax.ppermute(value, axis, pairs)


def kernel_apply(own_x, own_square, cols, dim):
    col_x = cols[:, :dim]
    col_w = cols[:, dim:]
    cross = jnp.dot(
        own_x, col_x.T, precision=lax.Precision.HIGHEST, preferred_element_type=jnp.float32
    )
    dist = own_square[:, None] + jnp.sum(col_x * col_x, axis=1)[None, :] - 2.0 * cross
    weights = jnp.exp(-kernel_scale * dist)
    return jnp.dot(
        weights, col_w, precision=lax.Precision.HIGHEST, preferred_element_type=jnp.float32
    )


def per_device(points, probes, leaf):
    n_node = lax.axis_size("node")
    count_rows = points.shape[0]
    dim = points.shape[1]
    cap = 4 * count_rows // n_node
    slots = n_node * cap
    dest = leaf[:, 0]
    onehot = (dest[:, None] == jnp.arange(n_node, dtype=jnp.int32)[None, :]).astype(jnp.int32)
    before = jnp.cumsum(onehot, axis=0) - onehot
    slot = jnp.sum(before * onehot, axis=1)
    position = dest * cap + slot
    payload = jnp.concatenate([points, probes], axis=1)
    width = payload.shape[1]
    outgoing = (
        jnp.zeros((slots, width), jnp.float32).at[position].set(payload).reshape(n_node, cap, width)
    )
    arrived = lax.all_to_all(outgoing, "node", split_axis=0, concat_axis=0, tiled=True).reshape(
        slots, width
    )
    own_x = arrived[:, :dim]
    own_square = jnp.sum(own_x * own_x, axis=1)
    block = min(256, slots)
    empty = jnp.zeros((slots, width - dim), jnp.float32)
    mirrored = swapped(arrived, "node", 0)
    total = empty
    piece = lax.all_gather(mirrored, "slab", axis=0, tiled=True)
    stacked = piece.reshape(piece.shape[0] // block, block, width)

    def step(carry, cols):
        return (carry + kernel_apply(own_x, own_square, cols, dim), None)

    total, _ = lax.scan(step, total, stacked)
    returned = lax.all_to_all(
        total.reshape(n_node, cap, width - dim), "node", split_axis=0, concat_axis=0, tiled=True
    )
    return returned.reshape(slots, width - dim)[position]


def solution(mesh):
    placed = (P(("node", "slab"), None), P(("node", "slab"), None), P(("node", "slab"), None))
    return jax.shard_map(
        per_device, mesh=mesh, in_specs=placed, out_specs=P(("node", "slab"), None), check_vma=False
    )
```

profile of v0, /device:TPU:1, one launch (start us, length us, event | category | flops | bytes accessed | tf_op | source)
XLA Modules:
  0.0 168.3 jit_solution(14709740134515818437)
XLA Ops:
  9.8 1.5 scatter_custom_fusion
  11.5 41.3 %all_to_all.10 = f32[128,4,192]{2,1,0:T(4,128)S(1)} all-to-all(f32[128,4,192]{2,1,0:T(4,128)S(1)} %reshape.18), channel_id=1, replica_groups=mesh['node'=128,'slab'=4] {'node'}, dimensions={0} | all-to-all | bytes 786432 | tf_op jit(solution)/shard_map/all_to_all | solution.py:44
  53.0 2.2 %collective-permute-start = (f32[512,192]{1,0:T(8,128)S(1)}, f32[512,192]{1,0:T(8,128)S(1)}, u32[]{:S(2)}, u32[]{:S(2)}) collective-permute-start(f32[512,192]{1,0:T(8,128)S(1)} %reshape.19), channel_id=1, source_target_pairs={{0,4},{4,0},{8,12},{12,8},{16,20},{20,16},{24,28},{28,24},{32,36},... | collective-permute-start | bytes 1179656 | tf_op jit(solution)/shard_map/ppermute | solution.py:12
  55.2 9.8 %collective-permute-done = f32[512,192]{1,0:T(8,128)S(1)} collective-permute-done((f32[512,192]{1,0:T(8,128)S(1)}, f32[512,192]{1,0:T(8,128)S(1)}, u32[]{:S(2)}, u32[]{:S(2)}) %collective-permute-start) | collective-permute-done | bytes 393248 | tf_op jit(solution)/shard_map/ppermute | solution.py:12
  66.0 30.6 %all-gather.2.cloned.1.call-done = f32[2048,192]{1,0:T(8,128)} async-done(((f32[512,192]{1,0:T(8,128)}), f32[2048,192]{1,0:T(8,128)}) %all-gather.2.cloned.1.call-update) | async-done | bytes 1572880 | tf_op jit(solution)/shard_map/all_gather | solution.py:53
  96.6 31.3 %while.11 = (s32[]{:T(128)}, f32[512,128]{1,0:T(8,128)}, f32[512]{0:T(512)S(1)}, f32[8,256,192]{2,1,0:T(8,128)}, f32[512,64]{1,0:T(8,128)S(1)}, /*index=5*/s32[]{:T(128)}, s32[]{:T(128)}) while((s32[]{:T(128)}, f32[512,128]{1,0:T(8,128)}, f32[512]{0:T(512)S(1)}, f32[8,256,192]{2,1,0:T(8,128)}, f32[512,64]{1,0:T(8,128)S(1)}, ...), condition=%wide.region_6.7_spmd.clone, body=%wide.region_4.6_spmd.clone.sunk | while | flops 302677760 | bytes 2560091 | solution.py:59
  96.6 1.0 dynamic-slice_bitcast_fusion.2
  98.3 1.4 convolution_add_fusion.2
  99.7 1.0 dynamic-slice_bitcast_fusion.2
  101.4 2.3 %convolution_add_fusion.2 = f32[512,128]{1,0:T(8,128)} fusion(f32[512,256]{1,0:T(8,128)S(1)} %fusion.25, f32[512,128]{1,0:T(8,128)} %get-tuple-element.102, f32[256,192]{1,0:T(8,128)S(1)} %dynamic-slice_bitcast_fusion.2, pred[]{:T(512)S(6)} %compare.3), kind=kOutput, calls=%fused_computation.7.clone.1 | convolution fusion | flops 201457664 | bytes 1179649 | tf_op jit(solution)/shard_map/while/body/eval_jaxpr/dot_general | solution.py:23
  103.7 1.0 dynamic-slice_bitcast_fusion.2
  105.4 2.3 %convolution_add_fusion.2 = f32[512,128]{1,0:T(8,128)} fusion(f32[512,256]{1,0:T(8,128)S(1)} %fusion.25, f32[512,128]{1,0:T(8,128)} %get-tuple-element.102, f32[256,192]{1,0:T(8,128)S(1)} %dynamic-slice_bitcast_fusion.2, pred[]{:T(512)S(6)} %compare.3), kind=kOutput, calls=%fused_computation.7.clone.1 | convolution fusion | flops 201457664 | bytes 1179649 | tf_op jit(solution)/shard_map/while/body/eval_jaxpr/dot_general | solution.py:23
  107.7 1.0 dynamic-slice_bitcast_fusion.2
  109.5 2.3 %convolution_add_fusion.2 = f32[512,128]{1,0:T(8,128)} fusion(f32[512,256]{1,0:T(8,128)S(1)} %fusion.25, f32[512,128]{1,0:T(8,128)} %get-tuple-element.102, f32[256,192]{1,0:T(8,128)S(1)} %dynamic-slice_bitcast_fusion.2, pred[]{:T(512)S(6)} %compare.3), kind=kOutput, calls=%fused_computation.7.clone.1 | convolution fusion | flops 201457664 | bytes 1179649 | tf_op jit(solution)/shard_map/while/body/eval_jaxpr/dot_general | solution.py:23
  111.8 1.0 dynamic-slice_bitcast_fusion.2
  113.5 2.3 %convolution_add_fusion.2 = f32[512,128]{1,0:T(8,128)} fusion(f32[512,256]{1,0:T(8,128)S(1)} %fusion.25, f32[512,128]{1,0:T(8,128)} %get-tuple-element.102, f32[256,192]{1,0:T(8,128)S(1)} %dynamic-slice_bitcast_fusion.2, pred[]{:T(512)S(6)} %compare.3), kind=kOutput, calls=%fused_computation.7.clone.1 | convolution fusion | flops 201457664 | bytes 1179649 | tf_op jit(solution)/shard_map/while/body/eval_jaxpr/dot_general | solution.py:23
  115.8 1.0 dynamic-slice_bitcast_fusion.2
  117.5 2.3 %convolution_add_fusion.2 = f32[512,128]{1,0:T(8,128)} fusion(f32[512,256]{1,0:T(8,128)S(1)} %fusion.25, f32[512,128]{1,0:T(8,128)} %get-tuple-element.102, f32[256,192]{1,0:T(8,128)S(1)} %dynamic-slice_bitcast_fusion.2, pred[]{:T(512)S(6)} %compare.3), kind=kOutput, calls=%fused_computation.7.clone.1 | convolution fusion | flops 201457664 | bytes 1179649 | tf_op jit(solution)/shard_map/while/body/eval_jaxpr/dot_general | solution.py:23
  119.8 1.0 dynamic-slice_bitcast_fusion.2
  121.5 2.3 %convolution_add_fusion.2 = f32[512,128]{1,0:T(8,128)} fusion(f32[512,256]{1,0:T(8,128)S(1)} %fusion.25, f32[512,128]{1,0:T(8,128)} %get-tuple-element.102, f32[256,192]{1,0:T(8,128)S(1)} %dynamic-slice_bitcast_fusion.2, pred[]{:T(512)S(6)} %compare.3), kind=kOutput, calls=%fused_computation.7.clone.1 | convolution fusion | flops 201457664 | bytes 1179649 | tf_op jit(solution)/shard_map/while/body/eval_jaxpr/dot_general | solution.py:23
  125.6 2.3 %convolution_add_fusion.2 = f32[512,128]{1,0:T(8,128)} fusion(f32[512,256]{1,0:T(8,128)S(1)} %fusion.25, f32[512,128]{1,0:T(8,128)} %get-tuple-element.102, f32[256,192]{1,0:T(8,128)S(1)} %dynamic-slice_bitcast_fusion.2, pred[]{:T(512)S(6)} %compare.3), kind=kOutput, calls=%fused_computation.7.clone.1 | convolution fusion | flops 201457664 | bytes 1179649 | tf_op jit(solution)/shard_map/while/body/eval_jaxpr/dot_general | solution.py:23
  127.9 15.7 %all-to-all-start.1 = ((f32[128,4,128]{2,1,0:T(4,128)}), f32[128,4,128]{2,1,0:T(4,128)S(1)}, u32[]{:S(2)}, u32[]{:S(2)}) async-start(f32[128,4,128]{2,1,0:T(4,128)} %bitcast.4), calls=%async_computation.1 | async-start | bytes 524288 | tf_op jit(solution)/shard_map/all_to_all | solution.py:60
  143.6 16.5 %all-to-all-done.1 = f32[128,4,128]{2,1,0:T(4,128)S(1)} async-done(((f32[128,4,128]{2,1,0:T(4,128)}), f32[128,4,128]{2,1,0:T(4,128)S(1)}, u32[]{:S(2)}, u32[]{:S(2)}) %all-to-all-start.1) | async-done | bytes 262176 | tf_op jit(solution)/shard_map/all_to_all | solution.py:60
  160.2 1.2 gather_fusion
  (31 shorter events, 11.3 us)
Async XLA Ops:
  6.5 90.1 %all-gather.2.cloned.1.call-start = ((), (), s32[]{:S(2)}) async-start(), calls=%async_computation.2 | async-start | bytes 2621440 | tf_op jit(solution)/shard_map/all_gather | solution.py:53
  53.0 12.0 %collective-permute-start = (f32[512,192]{1,0:T(8,128)S(1)}, f32[512,192]{1,0:T(8,128)S(1)}, u32[]{:S(2)}, u32[]{:S(2)}) collective-permute-start(f32[512,192]{1,0:T(8,128)S(1)} %reshape.19), channel_id=1, source_target_pairs={{0,4},{4,0},{8,12},{12,8},{16,20},{20,16},{24,28},{28,24},{32,36},... | collective-permute-start | bytes 1179656 | tf_op jit(solution)/shard_map/ppermute | solution.py:12
  65.0 0.8 copy-start
  127.9 32.3 %all-to-all-start.1 = ((f32[128,4,128]{2,1,0:T(4,128)}), f32[128,4,128]{2,1,0:T(4,128)S(1)}, u32[]{:S(2)}, u32[]{:S(2)}) async-start(f32[128,4,128]{2,1,0:T(4,128)} %bitcast.4), calls=%async_computation.1 | async-start | bytes 524288 | tf_op jit(solution)/shard_map/all_to_all | solution.py:60
Sparse Core Ops, SparseCore 0:
  65.9 30.6 all-gather.1
where the time goes:
time: 169 us; the launch traced here: 168 us
  waiting for transfers between devices  57 us (34%)
  blocking collectives  41.3 us (24%)
  matrix products  22.6 us (13%)
  starting transfers between devices  17.9 us (11%)
  between operations  13.5 us (8%)
  local copies, waits for them, and re-layouts  11 us (7%)
  other arithmetic  4.92 us (3%)
    all_to_all x1, blocking collectives, per_device(): lax.all_to_all(outgoing, 'node', split_axis=0, concat_axis=0, tiled=True)  41.3 us
    all_gather x1, waiting for transfers between devices, per_device(): piece = lax.all_gather(mirrored, 'slab', axis=0, tiled=True)  30.6 us
    dot_general x8, matrix products, kernel_apply(): jnp.dot(weights, col_w, precision=lax.Precision.HIGHEST, preferred_elemen...  17.6 us
    all_to_all x1, waiting for transfers between devices, per_device(): lax.all_to_all(total.reshape(n_node, cap, width - dim), 'node', split_axi...  16.5 us
    all_to_all x1, starting transfers between devices, per_device(): lax.all_to_all(total.reshape(n_node, cap, width - dim), 'node', split_axi...  15.7 us
    ppermute x1, waiting for transfers between devices, swapped(): return lax.ppermute(value, axis, pairs)  9.81 us
    squeeze x8, local copies, waits for them, and re-layouts, per_device(): total, _ = lax.scan(step, total, stacked)  7.73 us
    dot_general x8, matrix products, kernel_apply(): jnp.dot(own_x, col_x.T, precision=lax.Precision.HIGHEST, preferred_elemen...  5 us
  transfers between devices with their start and end apart: 3, of which 3 were waited for; matrix products, arithmetic and copies ran while one was open for 0% of the time, Pallas kernels for 0%

commit v1 on v0

v1 whole, which is shorter than its diff:
```python
import functools
import math

import jax
import jax.numpy as jnp
from jax import lax
from jax.experimental import pallas as pl
from jax.experimental.pallas import tpu as pltpu
from jax.sharding import PartitionSpec as P

kernel_scale = 1.0 / 64.0
log2_scale = kernel_scale * math.log2(math.e)
CAP = 4
UNIT = 6
LANES = 128


def split2(value):
    high = value.astype(jnp.bfloat16)
    low = (value - high.astype(jnp.float32)).astype(jnp.bfloat16)
    return high, low


def split3(value):
    high = value.astype(jnp.bfloat16)
    rest = value - high.astype(jnp.float32)
    mid = rest.astype(jnp.bfloat16)
    low = (rest - mid.astype(jnp.float32)).astype(jnp.bfloat16)
    return high, mid, low


def iota(shape, dim):
    return lax.broadcasted_iota(jnp.int32, shape, dim)


def nt(a, b):
    return lax.dot_general(a, b, (((1,), (1,)), ((), ())), preferred_element_type=jnp.float32)


def nn(a, b):
    return jnp.dot(a, b, preferred_element_type=jnp.float32)


def mask_bf16(mask):
    return jnp.where(mask, 1.0, 0.0).astype(jnp.bfloat16)


def pack_kernel(leaf_ref, xt_ref, w_ref, out_ref, pos_ref):
    n = leaf_ref.shape[1]
    dim = xt_ref.shape[0]
    leaf = leaf_ref[...]
    row = iota((LANES, n), 0)
    lane = iota((LANES, n), 1)
    own = row == leaf
    before = nn(mask_bf16(own), mask_bf16(row < lane))
    slot = jnp.sum(jnp.where(own, before, 0.0), axis=0, keepdims=True).astype(jnp.int32)
    pos_ref[...] = leaf * CAP + slot
    goal = jnp.bitwise_xor(leaf, 1) * CAP + slot
    choose = [mask_bf16(row * CAP == goal - j) for j in range(CAP)]
    w_parts = jnp.concatenate(split3(w_ref[...]), axis=1)
    for j in range(CAP):
        picked = nn(choose[j], w_parts)
        out_ref[pl.ds(j, LANES, stride=UNIT), :] = (
            picked[:, :LANES] + picked[:, LANES : 2 * LANES] + picked[:, 2 * LANES :]
        )
    empty = jnp.zeros((dim, n), jnp.bfloat16)
    x_parts = []
    for part in split3(xt_ref[...]):
        x_parts.append(jnp.concatenate([part, empty], axis=1))
        x_parts.append(jnp.concatenate([empty, part], axis=1))
    x_parts = jnp.concatenate(x_parts, axis=0)
    for h in range(CAP // 2):
        picked = nt(jnp.concatenate([choose[2 * h], choose[2 * h + 1]], axis=1), x_parts)
        out_ref[pl.ds(CAP + h, LANES, stride=UNIT), :] = (
            picked[:, :LANES] + picked[:, LANES : 2 * LANES] + picked[:, 2 * LANES :]
        )


def doubled(pair):
    turned = pltpu.roll(pair, 64, 1)
    low = iota(pair.shape, 1) < 64
    return jnp.concatenate([jnp.where(low, pair, turned), jnp.where(low, turned, pair)], axis=0)


def square_parts(x):
    total = jnp.sum(x * x, axis=1, keepdims=True) * (-0.5 * log2_scale)
    return [part.astype(jnp.float32) for part in split3(jnp.broadcast_to(total, x.shape))]


def left_operand(pair):
    x = doubled(pair)
    lane = iota(x.shape, 1)
    low = lane < 64
    s1, s2, s3 = square_parts(x)
    a1, a2, a3 = [part.astype(jnp.float32) for part in split3(x * (2.0 * log2_scale))]
    tail = jnp.where(lane < 3, 1.0, jnp.where(lane == 3, s1, jnp.where(lane == 4, s2, jnp.where(lane == 5, s3, 0.0))))
    parts = [a1, jnp.where(low, a2, a1), jnp.where(low, a3, a2), tail]
    return jnp.concatenate([part.astype(jnp.bfloat16) for part in parts], axis=1)


def right_operand(pair):
    x = doubled(pair)
    lane = iota(x.shape, 1)
    low = lane < 64
    s1, s2, s3 = square_parts(x)
    x1, x2, x3 = [part.astype(jnp.float32) for part in split3(x)]
    tail = jnp.where(lane == 0, s1, jnp.where(lane == 1, s2, jnp.where(lane == 2, s3, jnp.where(lane < 6, 1.0, 0.0))))
    first = jnp.where(low, x1, x2).astype(jnp.bfloat16)
    parts = [first, jnp.where(low, x1, x3).astype(jnp.bfloat16), first, tail.astype(jnp.bfloat16)]
    return jnp.concatenate(parts, axis=1)


def block_kernel(*refs, first, last):
    refs = list(refs)
    if first:
        own_ref = refs.pop(0)
    else:
        left_in, total_in = refs.pop(0), refs.pop(0)
    cols_ref = refs.pop(0)
    rows = LANES
    rights, values = [], []
    for h in range(CAP // 2):
        rights.append(right_operand(cols_ref[pl.ds(CAP + h, rows, stride=UNIT), :]))
        w = jnp.concatenate([cols_ref[pl.ds(2 * h + e, rows, stride=UNIT), :] for e in range(2)], axis=0)
        values.append(jnp.concatenate(split2(w), axis=1))
    if first:
        left_ref, total_ref = refs
        for h in range(CAP // 2):
            left_ref[pl.ds(2 * h * rows, 2 * rows), :] = left_operand(own_ref[pl.ds(h * rows, rows), :])
        source = left_ref
    else:
        (total_ref,) = refs
        source = left_in
    for j in range(CAP):
        left = source[pl.ds(j * rows, rows), :]
        total = None
        for h in range(CAP // 2):
            weights = jnp.exp2(nt(left, rights[h]))
            w1, w2 = split2(weights)
            part = nn(w1, values[h]) + nn(w2, values[h])
            total = part if total is None else total + part
        total = total[:, :LANES] + total[:, LANES:]
        if not first:
            total = total + total_in[pl.ds(j * rows, rows), :]
        if last:
            total_ref[pl.ds(j, rows, stride=CAP), :] = total
        else:
            total_ref[pl.ds(j * rows, rows), :] = total


def take_kernel(pos_ref, back_ref, out_ref):
    n = pos_ref.shape[1]
    slots = back_ref.shape[0]
    wanted = jnp.transpose(jnp.broadcast_to(pos_ref[...].astype(jnp.float32), (LANES, n))).astype(jnp.int32)
    lane = iota((n, LANES), 1)
    choose = jnp.concatenate([mask_bf16(wanted == lane + k * LANES) for k in range(slots // LANES)], axis=1)
    picked = nn(choose, jnp.concatenate(split3(back_ref[...]), axis=1))
    out_ref[...] = picked[:, :LANES] + picked[:, LANES : 2 * LANES] + picked[:, 2 * LANES :]


def coords_kernel(here_ref, out_ref):
    for h in range(CAP // 2):
        out_ref[pl.ds(h * LANES, LANES), :] = here_ref[pl.ds(CAP + h, LANES, stride=UNIT), :]


def whole(count):
    return [pl.BlockSpec(memory_space=pltpu.VMEM)] * count


def call(kernel, args, outs, flops):
    single = len(outs) == 1
    return pl.pallas_call(
        kernel,
        out_shape=outs[0] if single else outs,
        in_specs=whole(len(args)),
        out_specs=whole(1)[0] if single else whole(len(outs)),
        compiler_params=pltpu.CompilerParams(vmem_limit_bytes=24 * 1024 * 1024),
        cost_estimate=pl.CostEstimate(flops=flops, bytes_accessed=1 << 20, transcendentals=1 << 18),
    )(*args)


def swapped(value, axis, mask):
    pairs = [(source, source ^ mask) for source in range(lax.axis_size(axis))]
    return lax.ppermute(value, axis, pairs)


def per_device(points, probes, leaf):
    n_node = lax.axis_size("node")
    f32 = jnp.float32
    slots = n_node * CAP
    packed, pos = call(
        pack_kernel,
        (leaf.reshape(1, -1), points.T, probes),
        (jax.ShapeDtypeStruct((n_node * UNIT, LANES), f32), jax.ShapeDtypeStruct((1, leaf.shape[0]), jnp.int32)),
        1 << 28,
    )
    arrived = lax.all_to_all(
        packed.reshape(n_node, 1, UNIT * LANES), "node", split_axis=0, concat_axis=0, tiled=True
    )
    here = arrived.reshape(n_node * UNIT, LANES)
    far = swapped(here, "slab", 2)
    coords = call(coords_kernel, (here,), (jax.ShapeDtypeStruct((2 * n_node, LANES), f32),), 1 << 10)
    own = swapped(coords, "node", 1)
    beside = swapped(here, "slab", 1)
    total_shape = jax.ShapeDtypeStruct((slots, LANES), f32)
    flops = 1 << 31
    left, total = call(
        functools.partial(block_kernel, first=True, last=False),
        (own, here),
        (jax.ShapeDtypeStruct((slots, 4 * LANES), jnp.bfloat16), total_shape),
        flops,
    )
    middle = functools.partial(block_kernel, first=False, last=False)
    total = call(middle, (left, total, beside), (total_shape,), flops)
    far, total = lax.optimization_barrier((far, total))
    far_beside = swapped(far, "slab", 1)
    total = call(middle, (left, total, far), (total_shape,), flops)
    total = call(
        functools.partial(block_kernel, first=False, last=True), (left, total, far_beside), (total_shape,), flops
    )
    back = lax.all_to_all(
        total.reshape(n_node, CAP, LANES), "node", split_axis=0, concat_axis=0, tiled=True
    ).reshape(slots, LANES)
    return call(take_kernel, (pos, back), (jax.ShapeDtypeStruct(probes.shape, f32),), 1 << 27)


def solution(mesh):
    placed = (P(("node", "slab"), None), P(("node", "slab"), None), P(("node", "slab"), None))
    return jax.shard_map(
        per_device, mesh=mesh, in_specs=placed, out_specs=P(("node", "slab"), None), check_vma=False
    )
```

time: 169 us -> 91.7 us (0.54)
  waiting for transfers between devices: 57 us -> 4.8 us
  matrix products: 22.6 us -> 0 us
  blocking collectives: 41.3 us -> 61.1 us
  between operations: 13.5 us -> 0.1 us
  Pallas kernels: 0 us -> 9.92 us
  local copies, waits for them, and re-layouts: 11 us -> 2.25 us
  other arithmetic: 4.92 us -> 0 us
  starting transfers between devices: 17.9 us -> 13.2 us
    all_gather x1 -> x0, waiting for transfers between devices: 30.6 us -> none  [per_device(): piece = lax.all_gather(mirrored, 'slab', axis=0, tiled=True)]
    dot_general x16 -> x0, matrix products: 22.6 us -> none  [the longest x8 17.6 us: kernel_apply(): jnp.dot(weights, col_w, precision=lax.Precision.HIGHEST, preferred_elemen...]
    all_to_all x1 -> x2, blocking collectives: 41.3 us -> 61.1 us  [the longest x1 38.9 us: per_device(): lax.all_to_all(packed.reshape(n_node, 1, UNIT * LANES), 'node', split_axi...]
    all_to_all x1 -> x0, waiting for transfers between devices: 16.5 us -> none  [per_device(): lax.all_to_all(total.reshape(n_node, cap, width - dim), 'node', split_axi...]
    all_to_all x1 -> x0, starting transfers between devices: 15.7 us -> none  [per_device(): lax.all_to_all(total.reshape(n_node, cap, width - dim), 'node', split_axi...]
    ppermute x1 -> x4, starting transfers between devices: 2.17 us -> 13.2 us  [swapped(): return lax.ppermute(value, axis, pairs)]
    pallas_call x0 -> x7, Pallas kernels: none -> 9.92 us  [call(): pl.pallas_call(kernel, out_shape=outs[0] if single else outs, in_specs=wh...]
    squeeze x8 -> x0, local copies, waits for them, and re-layouts: 7.73 us -> none  [per_device(): total, _ = lax.scan(step, total, stacked)]
  transfers between devices with their start and end apart: 3 -> 4, of which waited for: 3 -> 2; matrix products, arithmetic and copies ran while one was open for 0% -> 0% of each run, Pallas kernels for 0% -> 7%
where the time goes in v1:
time: 91.7 us; the launch traced here: 91.3 us
  blocking collectives  61.1 us (67%)
  starting transfers between devices  13.2 us (14%)
  Pallas kernels  9.92 us (11%)
  waiting for transfers between devices  4.8 us (5%)
  local copies, waits for them, and re-layouts  2.25 us (2%)
    all_to_all x1, blocking collectives, per_device(): lax.all_to_all(packed.reshape(n_node, 1, UNIT * LANES), 'node', split_axi...  38.9 us
    all_to_all x1, blocking collectives, per_device(): lax.all_to_all(total.reshape(n_node, CAP, LANES), 'node', split_axis=0, c...  22.1 us
    ppermute x4, starting transfers between devices, swapped(): return lax.ppermute(value, axis, pairs)  13.2 us
    pallas_call x7, Pallas kernels, call(): pl.pallas_call(kernel, out_shape=outs[0] if single else outs, in_specs=wh...  9.92 us
    ppermute x4, waiting for transfers between devices, swapped(): return lax.ppermute(value, axis, pairs)  4.8 us
    unnamed x6, local copies, waits for them, and re-layouts  2.25 us
  transfers between devices with their start and end apart: 4, of which 2 were waited for; matrix products, arithmetic and copies ran while one was open for 0% of the time, Pallas kernels for 7%

profile of v1, /device:TPU:1, one launch (start us, length us, event | category | flops | bytes accessed | tf_op | source)
XLA Modules:
  0.0 91.3 jit_solution(2914215474185225871)
XLA Ops:
  0.0 0.0 copy-start.2
  0.0 0.7 copy-done.2
  0.7 0.0 copy-start
  0.7 0.8 copy-done
  1.5 0.0 copy-start.1
  1.5 0.8 copy-done.1
  2.3 0.5 shard_map.37
  2.8 38.9 %all_to_all.10 = f32[128,1,768]{2,1,0:T(1,128)S(1)} all-to-all(f32[128,1,768]{2,1,0:T(1,128)S(1)} %bitcast.10), channel_id=1, replica_groups=mesh['node'=128,'slab'=4] {'node'}, dimensions={0} | all-to-all | bytes 786432 | tf_op jit(solution)/shard_map/all_to_all | solution.py:197
  41.7 4.9 %collective-permute-start.2 = (f32[768,128]{1,0:T(8,128)S(1)}, f32[768,128]{1,0:T(8,128)S(1)}, u32[]{:S(2)}, u32[]{:S(2)}) collective-permute-start(f32[768,128]{1,0:T(8,128)S(1)} %bitcast.6), channel_id=1, source_target_pairs={{0,1},{1,0},{2,3},{3,2},{4,5},{5,4},{6,7},{7,6},{8,9},{9,8},{10,11... | collective-permute-start | bytes 1179656 | tf_op jit(solution)/shard_map/ppermute | solution.py:184
  46.6 2.2 %collective-permute-start = (f32[256,128]{1,0:T(8,128)S(1)}, f32[256,128]{1,0:T(8,128)S(1)}, u32[]{:S(2)}, u32[]{:S(2)}) collective-permute-start(f32[256,128]{1,0:T(8,128)S(1)} %shard_map.38), channel_id=1, source_target_pairs={{0,4},{4,0},{8,12},{12,8},{16,20},{20,16},{24,28},{28,24},{32,36},... | collective-permute-start | bytes 393224 | tf_op jit(solution)/shard_map/ppermute | solution.py:184
  48.8 3.1 %collective-permute-start.1 = (f32[768,128]{1,0:T(8,128)S(1)}, f32[768,128]{1,0:T(8,128)S(1)}, u32[]{:S(2)}, u32[]{:S(2)}) collective-permute-start(f32[768,128]{1,0:T(8,128)S(1)} %bitcast.8), channel_id=1, source_target_pairs={{0,2},{1,3},{2,0},{3,1},{4,6},{5,7},{6,4},{7,5},{8,10},{9,11},{10,... | collective-permute-start | bytes 1179656 | tf_op jit(solution)/shard_map/ppermute | solution.py:184
  51.9 1.7 %collective-permute-done.refs_0_ = f32[256,128]{1,0:T(8,128)S(1)} collective-permute-done((f32[256,128]{1,0:T(8,128)S(1)}, f32[256,128]{1,0:T(8,128)S(1)}, u32[]{:S(2)}, u32[]{:S(2)}) %collective-permute-start) | collective-permute-done | bytes 131104 | tf_op jit(solution)/shard_map/ppermute | solution.py:184
  53.6 2.3 %shard_map.39 = (bf16[512,512]{1,0:T(8,128)(2,1)S(1)}, f32[512,128]{1,0:T(8,128)S(1)}) custom-call(f32[256,128]{1,0:T(8,128)S(1)} %collective-permute-done.refs_0_, f32[768,128]{1,0:T(8,128)S(1)} %bitcast.9), custom_call_target="tpu_custom_call" | custom-call | flops 2147483648 | bytes 1048576 | tf_op jit(solution)/shard_map/pallas_call | solution.py:172
  55.9 0.0 collective-permute-done.2.refs_2_
  55.9 2.1 %shard_map.40.refs_1_ = f32[512,128]{1,0:T(8,128)S(1)} custom-call(bf16[512,512]{1,0:T(8,128)(2,1)S(1)} %get-tuple-element.13.refs_0_, f32[512,128]{1,0:T(8,128)S(1)} %get-tuple-element.14.refs_1_, f32[768,128]{1,0:T(8,128)S(1)} %collective-permute-done.2.refs_2_), custom_call_target="tpu_custom_call" | custom-call | flops 2147483648 | bytes 1048576 | tf_op jit(solution)/shard_map/pallas_call | solution.py:172
  58.0 3.1 %collective-permute-done.1.refs_2_ = f32[768,128]{1,0:T(8,128)S(1)} collective-permute-done((f32[768,128]{1,0:T(8,128)S(1)}, f32[768,128]{1,0:T(8,128)S(1)}, u32[]{:S(2)}, u32[]{:S(2)}) %collective-permute-start.1) | collective-permute-done | bytes 393248 | tf_op jit(solution)/shard_map/ppermute | solution.py:184
  61.1 3.0 %collective-permute-start.3 = (f32[768,128]{1,0:T(8,128)S(1)}, f32[768,128]{1,0:T(8,128)S(1)}, u32[]{:S(2)}, u32[]{:S(2)}) collective-permute-start(f32[768,128]{1,0:T(8,128)S(1)} %collective-permute-done.1.refs_2_), channel_id=1, source_target_pairs={{0,1},{1,0},{2,3},{3,2},{4,5},{5,4},{6,7},{7,6},{8,9},{9,8},{10,11... | collective-permute-start | bytes 1179656 | tf_op jit(solution)/shard_map/ppermute | solution.py:184
  64.1 2.1 %shard_map.41.refs_1_ = f32[512,128]{1,0:T(8,128)S(1)} custom-call(bf16[512,512]{1,0:T(8,128)(2,1)S(1)} %get-tuple-element.13.refs_0_, f32[512,128]{1,0:T(8,128)S(1)} %shard_map.40.refs_1_, f32[768,128]{1,0:T(8,128)S(1)} %collective-permute-done.1.refs_2_), custom_call_target="tpu_custom_call" | custom-call | flops 2147483648 | bytes 1048576 | tf_op jit(solution)/shard_map/pallas_call | solution.py:172
  66.2 0.0 collective-permute-done.3.refs_2_
  66.2 2.1 %shard_map.42 = f32[512,128]{1,0:T(8,128)S(1)} custom-call(bf16[512,512]{1,0:T(8,128)(2,1)S(1)} %get-tuple-element.13.refs_0_, f32[512,128]{1,0:T(8,128)S(1)} %shard_map.41.refs_1_, f32[768,128]{1,0:T(8,128)S(1)} %collective-permute-done.3.refs_2_), custom_call_target="tpu_custom_call" | custom-call | flops 2147483648 | bytes 1048576 | tf_op jit(solution)/shard_map/pallas_call | solution.py:172
  68.3 22.1 %all_to_all.11 = f32[128,4,128]{2,1,0:T(4,128)S(1)} all-to-all(f32[128,4,128]{2,1,0:T(4,128)S(1)} %bitcast.11), channel_id=1, replica_groups=mesh['node'=128,'slab'=4] {'node'}, dimensions={0} | all-to-all | bytes 524288 | tf_op jit(solution)/shard_map/all_to_all | solution.py:221
  90.4 0.9 shard_map.43
  (1 shorter events, 0.0 us)
Async XLA Ops:
  0.0 0.7 copy-start.2
  0.7 0.8 copy-start
  1.5 0.8 copy-start.1
  41.7 14.2 %collective-permute-start.2 = (f32[768,128]{1,0:T(8,128)S(1)}, f32[768,128]{1,0:T(8,128)S(1)}, u32[]{:S(2)}, u32[]{:S(2)}) collective-permute-start(f32[768,128]{1,0:T(8,128)S(1)} %bitcast.6), channel_id=1, source_target_pairs={{0,1},{1,0},{2,3},{3,2},{4,5},{5,4},{6,7},{7,6},{8,9},{9,8},{10,11... | collective-permute-start | bytes 1179656 | tf_op jit(solution)/shard_map/ppermute | solution.py:184
  46.6 7.0 %collective-permute-start = (f32[256,128]{1,0:T(8,128)S(1)}, f32[256,128]{1,0:T(8,128)S(1)}, u32[]{:S(2)}, u32[]{:S(2)}) collective-permute-start(f32[256,128]{1,0:T(8,128)S(1)} %shard_map.38), channel_id=1, source_target_pairs={{0,4},{4,0},{8,12},{12,8},{16,20},{20,16},{24,28},{28,24},{32,36},... | collective-permute-start | bytes 393224 | tf_op jit(solution)/shard_map/ppermute | solution.py:184
  48.8 12.3 %collective-permute-start.1 = (f32[768,128]{1,0:T(8,128)S(1)}, f32[768,128]{1,0:T(8,128)S(1)}, u32[]{:S(2)}, u32[]{:S(2)}) collective-permute-start(f32[768,128]{1,0:T(8,128)S(1)} %bitcast.8), channel_id=1, source_target_pairs={{0,2},{1,3},{2,0},{3,1},{4,6},{5,7},{6,4},{7,5},{8,10},{9,11},{10,... | collective-permute-start | bytes 1179656 | tf_op jit(solution)/shard_map/ppermute | solution.py:184
  61.1 5.1 %collective-permute-start.3 = (f32[768,128]{1,0:T(8,128)S(1)}, f32[768,128]{1,0:T(8,128)S(1)}, u32[]{:S(2)}, u32[]{:S(2)}) collective-permute-start(f32[768,128]{1,0:T(8,128)S(1)} %collective-permute-done.1.refs_2_), channel_id=1, source_target_pairs={{0,1},{1,0},{2,3},{3,2},{4,5},{5,4},{6,7},{7,6},{8,9},{9,8},{10,11... | collective-permute-start | bytes 1179656 | tf_op jit(solution)/shard_map/ppermute | solution.py:184

commit v2 on v1

--- a/solution.py
+++ b/solution.py
@@ -45,14 +45,25 @@
     return jnp.where(mask, 1.0, 0.0).astype(jnp.bfloat16)
 
 
-def pack_kernel(leaf_ref, xt_ref, w_ref, out_ref, pos_ref):
+def choose_kernel(pos_ref, choose_ref):
+    n = pos_ref.shape[1]
+    wanted = jnp.transpose(jnp.broadcast_to(pos_ref[...].astype(jnp.float32), (LANES, n))).astype(jnp.int32)
+    lane = iota((n, LANES), 1)
+    for k in range(choose_ref.shape[1] // LANES):
+        choose_ref[:, k * LANES : (k + 1) * LANES] = mask_bf16(wanted == lane + k * LANES)
+
+
+def earlier_kernel(out_ref):
+    out_ref[...] = mask_bf16(iota(out_ref.shape, 0) < iota(out_ref.shape, 1))
+
+
+def pack_kernel(earlier_ref, leaf_ref, xt_ref, w_ref, out_ref, pos_ref):
     n = leaf_ref.shape[1]
     dim = xt_ref.shape[0]
     leaf = leaf_ref[...]
     row = iota((LANES, n), 0)
-    lane = iota((LANES, n), 1)
     own = row == leaf
-    before = nn(mask_bf16(own), mask_bf16(row < lane))
+    before = nn(mask_bf16(own), earlier_ref[...])
     slot = jnp.sum(jnp.where(own, before, 0.0), axis=0, keepdims=True).astype(jnp.int32)
     pos_ref[...] = leaf * CAP + slot
     goal = jnp.bitwise_xor(leaf, 1) * CAP + slot
@@ -131,30 +142,24 @@
     else:
         (total_ref,) = refs
         source = left_in
-    for j in range(CAP):
-        left = source[pl.ds(j * rows, rows), :]
-        total = None
-        for h in range(CAP // 2):
-            weights = jnp.exp2(nt(left, rights[h]))
-            w1, w2 = split2(weights)
-            part = nn(w1, values[h]) + nn(w2, values[h])
-            total = part if total is None else total + part
-        total = total[:, :LANES] + total[:, LANES:]
-        if not first:
-            total = total + total_in[pl.ds(j * rows, rows), :]
-        if last:
-            total_ref[pl.ds(j, rows, stride=CAP), :] = total
-        else:
-            total_ref[pl.ds(j * rows, rows), :] = total
-
-
-def take_kernel(pos_ref, back_ref, out_ref):
-    n = pos_ref.shape[1]
-    slots = back_ref.shape[0]
-    wanted = jnp.transpose(jnp.broadcast_to(pos_ref[...].astype(jnp.float32), (LANES, n))).astype(jnp.int32)
-    lane = iota((n, LANES), 1)
-    choose = jnp.concatenate([mask_bf16(wanted == lane + k * LANES) for k in range(slots // LANES)], axis=1)
-    picked = nn(choose, jnp.concatenate(split3(back_ref[...]), axis=1))
+    left = source[...]
+    total = None
+    for h in range(CAP // 2):
+        w1, w2 = split2(jnp.exp2(nt(left, rights[h])))
+        part = nn(w1, values[h]) + nn(w2, values[h])
+        total = part if total is None else total + part
+    total = total[:, :LANES] + total[:, LANES:]
+    if not first:
+        total = total + total_in[...]
+    if last:
+        for j in range(CAP):
+            total_ref[pl.ds(j, rows, stride=CAP), :] = total[j * rows : (j + 1) * rows, :]
+    else:
+        total_ref[...] = total
+
+
+def take_kernel(choose_ref, back_ref, out_ref):
+    picked = nn(choose_ref[...], jnp.concatenate(split3(back_ref[...]), axis=1))
     out_ref[...] = picked[:, :LANES] + picked[:, LANES : 2 * LANES] + picked[:, 2 * LANES :]
 
 
@@ -175,7 +180,7 @@
         in_specs=whole(len(args)),
         out_specs=whole(1)[0] if single else whole(len(outs)),
         compiler_params=pltpu.CompilerParams(vmem_limit_bytes=24 * 1024 * 1024),
-        cost_estimate=pl.CostEstimate(flops=flops, bytes_accessed=1 << 20, transcendentals=1 << 18),
+        cost_estimate=pl.CostEstimate(flops=flops, bytes_accessed=1 << 10, transcendentals=0),
     )(*args)
 
 
@@ -188,9 +193,11 @@
     n_node = lax.axis_size("node")
     f32 = jnp.float32
     slots = n_node * CAP
+    bf16 = jnp.bfloat16
+    earlier = call(earlier_kernel, (), (jax.ShapeDtypeStruct((LANES, leaf.shape[0]), bf16),), 1 << 33)
     packed, pos = call(
         pack_kernel,
-        (leaf.reshape(1, -1), points.T, probes),
+        (earlier, leaf.reshape(1, -1), points.T, probes),
         (jax.ShapeDtypeStruct((n_node * UNIT, LANES), f32), jax.ShapeDtypeStruct((1, leaf.shape[0]), jnp.int32)),
         1 << 28,
     )
@@ -203,7 +210,7 @@
     own = swapped(coords, "node", 1)
     beside = swapped(here, "slab", 1)
     total_shape = jax.ShapeDtypeStruct((slots, LANES), f32)
-    flops = 1 << 31
+    flops = 1 << 12
     left, total = call(
         functools.partial(block_kernel, first=True, last=False),
         (own, here),
@@ -211,17 +218,18 @@
         flops,
     )
     middle = functools.partial(block_kernel, first=False, last=False)
-    total = call(middle, (left, total, beside), (total_shape,), flops)
-    far, total = lax.optimization_barrier((far, total))
+    choose = call(choose_kernel, (pos,), (jax.ShapeDtypeStruct((leaf.shape[0], slots), bf16),), 1 << 12)
+    far, total, choose = lax.optimization_barrier((far, total, choose))
     far_beside = swapped(far, "slab", 1)
     total = call(middle, (left, total, far), (total_shape,), flops)
+    total = call(middle, (left, total, beside), (total_shape,), flops)
     total = call(
         functools.partial(block_kernel, first=False, last=True), (left, total, far_beside), (total_shape,), flops
     )
     back = lax.all_to_all(
         total.reshape(n_node, CAP, LANES), "node", split_axis=0, concat_axis=0, tiled=True
     ).reshape(slots, LANES)
-    return call(take_kernel, (pos, back), (jax.ShapeDtypeStruct(probes.shape, f32),), 1 << 27)
+    return call(take_kernel, (choose, back), (jax.ShapeDtypeStruct(probes.shape, f32),), 1 << 27)
 
 
 def solution(mesh):

time: 91.7 us -> 83.4 us (0.909)
  waiting for transfers between devices: 4.8 us -> 0.01 us
  Pallas kernels: 9.92 us -> 6.04 us
  starting transfers between devices: 13.2 us -> 15 us
  local copies, waits for them, and re-layouts: 2.25 us -> 0.84 us
    ppermute x4, waiting for transfers between devices: 4.8 us -> 0.01 us  [swapped(): return lax.ppermute(value, axis, pairs)]
    pallas_call x7 -> x9, Pallas kernels: 9.92 us -> 6.04 us  [call(): pl.pallas_call(kernel, out_shape=outs[0] if single else outs, in_specs=wh...]
    ppermute x4, starting transfers between devices: 13.2 us -> 15 us  [swapped(): return lax.ppermute(value, axis, pairs)]
    unnamed x6, local copies, waits for them, and re-layouts: 2.25 us -> 0.84 us
  transfers between devices with their start and end apart: 4 -> 4, of which waited for: 2 -> 0; matrix products, arithmetic and copies ran while one was open for 0% -> 0% of each run, Pallas kernels for 7% -> 4%
where the time goes in v2:
time: 83.4 us; the launch traced here: 83.1 us
  blocking collectives  61.1 us (73%)
  starting transfers between devices  15 us (18%)
  Pallas kernels  6.04 us (7%)
  local copies, waits for them, and re-layouts  0.84 us (1%)
    all_to_all x1, blocking collectives, per_device(): lax.all_to_all(packed.reshape(n_node, 1, UNIT * LANES), 'node', split_axi...  38.9 us
    all_to_all x1, blocking collectives, per_device(): lax.all_to_all(total.reshape(n_node, CAP, LANES), 'node', split_axis=0, c...  22.2 us
    ppermute x4, starting transfers between devices, swapped(): return lax.ppermute(value, axis, pairs)  15 us
    pallas_call x9, Pallas kernels, call(): pl.pallas_call(kernel, out_shape=outs[0] if single else outs, in_specs=wh...  6.04 us
  transfers between devices with their start and end apart: 4, of which 0 were waited for; matrix products, arithmetic and copies ran while one was open for 0% of the time, Pallas kernels for 4%

profile of v2, /device:TPU:1, one launch (start us, length us, event | category | flops | bytes accessed | tf_op | source)
XLA Modules:
  0.0 83.1 jit_solution(13268559214903700033)
XLA Ops:
  0.0 0.0 copy-start.1
  0.0 0.0 copy-start
  0.0 0.0 copy-start.2
  0.0 0.7 copy-done.1
  0.8 0.1 copy-done
  0.9 0.0 copy-done.2
  0.9 0.5 shard_map.38
  1.4 38.9 %all_to_all.10 = f32[128,1,768]{2,1,0:T(1,128)S(1)} all-to-all(f32[128,1,768]{2,1,0:T(1,128)S(1)} %bitcast.11), channel_id=1, replica_groups=mesh['node'=128,'slab'=4] {'node'}, dimensions={0} | all-to-all | bytes 786432 | tf_op jit(solution)/shard_map/all_to_all | solution.py:204
  40.3 3.1 %collective-permute-start = (f32[768,128]{1,0:T(8,128)S(1)}, f32[768,128]{1,0:T(8,128)S(1)}, u32[]{:S(2)}, u32[]{:S(2)}) collective-permute-start(f32[768,128]{1,0:T(8,128)S(1)} %bitcast.6), channel_id=1, source_target_pairs={{0,2},{1,3},{2,0},{3,1},{4,6},{5,7},{6,4},{7,5},{8,10},{9,11},{10,... | collective-permute-start | bytes 1179656 | tf_op jit(solution)/shard_map/ppermute | solution.py:189
  43.4 2.2 %collective-permute-start.1 = (f32[256,128]{1,0:T(8,128)S(1)}, f32[256,128]{1,0:T(8,128)S(1)}, u32[]{:S(2)}, u32[]{:S(2)}) collective-permute-start(f32[256,128]{1,0:T(8,128)S(1)} %shard_map.39), channel_id=1, source_target_pairs={{0,4},{4,0},{8,12},{12,8},{16,20},{20,16},{24,28},{28,24},{32,36},... | collective-permute-start | bytes 393224 | tf_op jit(solution)/shard_map/ppermute | solution.py:189
  45.6 0.1 shard_map.41.choose_ref
  45.7 5.6 %collective-permute-start.2 = (f32[768,128]{1,0:T(8,128)S(1)}, f32[768,128]{1,0:T(8,128)S(1)}, u32[]{:S(2)}, u32[]{:S(2)}) collective-permute-start(f32[768,128]{1,0:T(8,128)S(1)} %bitcast.8), channel_id=1, source_target_pairs={{0,1},{1,0},{2,3},{3,2},{4,5},{5,4},{6,7},{7,6},{8,9},{9,8},{10,11... | collective-permute-start | bytes 1179656 | tf_op jit(solution)/shard_map/ppermute | solution.py:189
  51.3 0.0 collective-permute-done.1.refs_0_
  51.3 1.2 %shard_map.40 = (bf16[512,512]{1,0:T(8,128)(2,1)S(1)}, f32[512,128]{1,0:T(8,128)S(1)}) custom-call(f32[256,128]{1,0:T(8,128)S(1)} %collective-permute-done.1.refs_0_, f32[768,128]{1,0:T(8,128)S(1)} %bitcast.9), custom_call_target="tpu_custom_call" | custom-call | flops 4096 | bytes 1024 | tf_op jit(solution)/shard_map/pallas_call | solution.py:177
  52.5 0.0 collective-permute-done.refs_2_
  52.6 4.2 %collective-permute-start.3 = (f32[768,128]{1,0:T(8,128)S(1)}, f32[768,128]{1,0:T(8,128)S(1)}, u32[]{:S(2)}, u32[]{:S(2)}) collective-permute-start(f32[768,128]{1,0:T(8,128)S(1)} %collective-permute-done.refs_2_), channel_id=1, source_target_pairs={{0,1},{1,0},{2,3},{3,2},{4,5},{5,4},{6,7},{7,6},{8,9},{9,8},{10,11... | collective-permute-start | bytes 1179656 | tf_op jit(solution)/shard_map/ppermute | solution.py:189
  56.7 1.1 %shard_map.42.refs_1_ = f32[512,128]{1,0:T(8,128)S(1)} custom-call(bf16[512,512]{1,0:T(8,128)(2,1)S(1)} %get-tuple-element.16.refs_0_, f32[512,128]{1,0:T(8,128)S(1)} %get-tuple-element.17.refs_1_, f32[768,128]{1,0:T(8,128)S(1)} %collective-permute-done.refs_2_), custom_call_target="tpu_custom_call" | custom-call | flops 4096 | bytes 1024 | tf_op jit(solution)/shard_map/pallas_call | solution.py:177
  57.8 0.0 collective-permute-done.2.refs_2_
  57.9 1.1 %shard_map.43.refs_1_ = f32[512,128]{1,0:T(8,128)S(1)} custom-call(bf16[512,512]{1,0:T(8,128)(2,1)S(1)} %get-tuple-element.16.refs_0_, f32[512,128]{1,0:T(8,128)S(1)} %shard_map.42.refs_1_, f32[768,128]{1,0:T(8,128)S(1)} %collective-permute-done.2.refs_2_), custom_call_target="tpu_custom_call" | custom-call | flops 4096 | bytes 1024 | tf_op jit(solution)/shard_map/pallas_call | solution.py:177
  59.0 0.0 collective-permute-done.3.refs_2_
  59.0 1.1 %shard_map.44 = f32[512,128]{1,0:T(8,128)S(1)} custom-call(bf16[512,512]{1,0:T(8,128)(2,1)S(1)} %get-tuple-element.16.refs_0_, f32[512,128]{1,0:T(8,128)S(1)} %shard_map.43.refs_1_, f32[768,128]{1,0:T(8,128)S(1)} %collective-permute-done.3.refs_2_), custom_call_target="tpu_custom_call" | custom-call | flops 4096 | bytes 1024 | tf_op jit(solution)/shard_map/pallas_call | solution.py:177
  60.1 22.2 %all_to_all.11 = f32[128,4,128]{2,1,0:T(4,128)S(1)} all-to-all(f32[128,4,128]{2,1,0:T(4,128)S(1)} %bitcast.10), channel_id=1, replica_groups=mesh['node'=128,'slab'=4] {'node'}, dimensions={0} | all-to-all | bytes 524288 | tf_op jit(solution)/shard_map/all_to_all | solution.py:229
  82.2 0.9 %shard_map.45 = f32[128,128]{1,0:T(8,128)} custom-call(bf16[128,512]{1,0:T(8,128)(2,1)S(1)} %shard_map.41.choose_ref, f32[512,128]{1,0:T(8,128)S(1)} %bitcast.12), custom_call_target="tpu_custom_call" | custom-call | flops 134217728 | bytes 1024 | tf_op jit(solution)/shard_map/pallas_call | solution.py:177
  (2 shorter events, 0.0 us)
Async XLA Ops:
  0.0 0.8 copy-start.1
  0.0 0.9 %copy-start = (f32[128,128]{1,0:T(8,128)S(1)}, f32[128,128]{1,0:T(8,128)}, u32[]{:S(2)}) copy-start(f32[128,128]{1,0:T(8,128)} %w_ref.1) | copy-start | bytes 196612
  0.0 0.8 %copy-start.2 = (s32[128,1]{0,1:T(1,128)S(1)}, s32[128,1]{0,1:T(1,128)}, u32[]{:S(2)}) copy-start(s32[128,1]{0,1:T(1,128)} %param.5) | copy-start | bytes 1540
  40.3 12.2 %collective-permute-start = (f32[768,128]{1,0:T(8,128)S(1)}, f32[768,128]{1,0:T(8,128)S(1)}, u32[]{:S(2)}, u32[]{:S(2)}) collective-permute-start(f32[768,128]{1,0:T(8,128)S(1)} %bitcast.6), channel_id=1, source_target_pairs={{0,2},{1,3},{2,0},{3,1},{4,6},{5,7},{6,4},{7,5},{8,10},{9,11},{10,... | collective-permute-start | bytes 1179656 | tf_op jit(solution)/shard_map/ppermute | solution.py:189
  43.4 7.9 %collective-permute-start.1 = (f32[256,128]{1,0:T(8,128)S(1)}, f32[256,128]{1,0:T(8,128)S(1)}, u32[]{:S(2)}, u32[]{:S(2)}) collective-permute-start(f32[256,128]{1,0:T(8,128)S(1)} %shard_map.39), channel_id=1, source_target_pairs={{0,4},{4,0},{8,12},{12,8},{16,20},{20,16},{24,28},{28,24},{32,36},... | collective-permute-start | bytes 393224 | tf_op jit(solution)/shard_map/ppermute | solution.py:189
  45.7 12.1 %collective-permute-start.2 = (f32[768,128]{1,0:T(8,128)S(1)}, f32[768,128]{1,0:T(8,128)S(1)}, u32[]{:S(2)}, u32[]{:S(2)}) collective-permute-start(f32[768,128]{1,0:T(8,128)S(1)} %bitcast.8), channel_id=1, source_target_pairs={{0,1},{1,0},{2,3},{3,2},{4,5},{5,4},{6,7},{7,6},{8,9},{9,8},{10,11... | collective-permute-start | bytes 1179656 | tf_op jit(solution)/shard_map/ppermute | solution.py:189
  52.6 6.4 %collective-permute-start.3 = (f32[768,128]{1,0:T(8,128)S(1)}, f32[768,128]{1,0:T(8,128)S(1)}, u32[]{:S(2)}, u32[]{:S(2)}) collective-permute-start(f32[768,128]{1,0:T(8,128)S(1)} %collective-permute-done.refs_2_), channel_id=1, source_target_pairs={{0,1},{1,0},{2,3},{3,2},{4,5},{5,4},{6,7},{7,6},{8,9},{9,8},{10,11... | collective-permute-start | bytes 1179656 | tf_op jit(solution)/shard_map/ppermute | solution.py:189

commit v3 on v2

--- a/solution.py
+++ b/solution.py
@@ -13,6 +13,7 @@
 CAP = 4
 UNIT = 6
 LANES = 128
+NODE_Y, NODE_Z, NODE_X = 8, 4, 4
 
 
 def split2(value):
@@ -55,6 +56,12 @@
 
 def earlier_kernel(out_ref):
     out_ref[...] = mask_bf16(iota(out_ref.shape, 0) < iota(out_ref.shape, 1))
+
+
+def place(node):
+    x = jnp.bitwise_and(node, NODE_X - 1)
+    z = jnp.bitwise_and(node // NODE_X, NODE_Z - 1)
+    return (x * NODE_Z + z) * NODE_Y + node // (NODE_X * NODE_Z)
 
 
 def pack_kernel(earlier_ref, leaf_ref, xt_ref, w_ref, out_ref, pos_ref):
@@ -65,8 +72,8 @@
     own = row == leaf
     before = nn(mask_bf16(own), earlier_ref[...])
     slot = jnp.sum(jnp.where(own, before, 0.0), axis=0, keepdims=True).astype(jnp.int32)
-    pos_ref[...] = leaf * CAP + slot
-    goal = jnp.bitwise_xor(leaf, 1) * CAP + slot
+    pos_ref[...] = place(leaf) * CAP + slot
+    goal = place(jnp.bitwise_xor(leaf, 1)) * CAP + slot
     choose = [mask_bf16(row * CAP == goal - j) for j in range(CAP)]
     w_parts = jnp.concatenate(split3(w_ref[...]), axis=1)
     for j in range(CAP):
@@ -143,12 +150,12 @@
         (total_ref,) = refs
         source = left_in
     left = source[...]
-    total = None
+    main, rest = 0.0, 0.0
     for h in range(CAP // 2):
         w1, w2 = split2(jnp.exp2(nt(left, rights[h])))
-        part = nn(w1, values[h]) + nn(w2, values[h])
-        total = part if total is None else total + part
-    total = total[:, :LANES] + total[:, LANES:]
+        main = main + nn(w1, values[h])
+        rest = rest + nn(w2, values[h][:, :LANES])
+    total = main[:, :LANES] + (main[:, LANES:] + rest)
     if not first:
         total = total + total_in[...]
     if last:
@@ -182,6 +189,11 @@
         compiler_params=pltpu.CompilerParams(vmem_limit_bytes=24 * 1024 * 1024),
         cost_estimate=pl.CostEstimate(flops=flops, bytes_accessed=1 << 10, transcendentals=0),
     )(*args)
+
+
+def exchanged(value):
+    order = [(y * NODE_Z + z) * NODE_X + x for x in range(NODE_X) for z in range(NODE_Z) for y in range(NODE_Y)]
+    return lax.all_to_all(value, "node", split_axis=0, concat_axis=0, axis_index_groups=[order], tiled=True)
 
 
 def swapped(value, axis, mask):
@@ -201,9 +213,7 @@
         (jax.ShapeDtypeStruct((n_node * UNIT, LANES), f32), jax.ShapeDtypeStruct((1, leaf.shape[0]), jnp.int32)),
         1 << 28,
     )
-    arrived = lax.all_to_all(
-        packed.reshape(n_node, 1, UNIT * LANES), "node", split_axis=0, concat_axis=0, tiled=True
-    )
+    arrived = exchanged(packed.reshape(n_node, 1, UNIT * LANES))
     here = arrived.reshape(n_node * UNIT, LANES)
     far = swapped(here, "slab", 2)
     coords = call(coords_kernel, (here,), (jax.ShapeDtypeStruct((2 * n_node, LANES), f32),), 1 << 10)
@@ -226,9 +236,7 @@
     total = call(
         functools.partial(block_kernel, first=False, last=True), (left, total, far_beside), (total_shape,), flops
     )
-    back = lax.all_to_all(
-        total.reshape(n_node, CAP, LANES), "node", split_axis=0, concat_axis=0, tiled=True
-    ).reshape(slots, LANES)
+    back = exchanged(total.reshape(n_node, CAP, LANES)).reshape(slots, LANES)
     return call(take_kernel, (choose, back), (jax.ShapeDtypeStruct(probes.shape, f32),), 1 << 27)
 
 

time: 83.4 us -> 81.7 us (0.980)
  no operation moved by 1% of the time
where the time goes in v3:
time: 81.7 us; the launch traced here: 81.4 us
  blocking collectives  60.6 us (74%)
  starting transfers between devices  14.6 us (18%)
  Pallas kernels  5.23 us (6%)
  local copies, waits for them, and re-layouts  0.84 us (1%)
    all_to_all x2, blocking collectives, exchanged(): lax.all_to_all(value, 'node', split_axis=0, concat_axis=0, axis_index_gro...  60.6 us
    ppermute x4, starting transfers between devices, swapped(): return lax.ppermute(value, axis, pairs)  14.6 us
    pallas_call x9, Pallas kernels, call(): pl.pallas_call(kernel, out_shape=outs[0] if single else outs, in_specs=wh...  5.23 us
  transfers between devices with their start and end apart: 4, of which 0 were waited for; matrix products, arithmetic and copies ran while one was open for 0% of the time, Pallas kernels for 4%

profile of v3, /device:TPU:1, one launch (start us, length us, event | category | flops | bytes accessed | tf_op | source)
XLA Modules:
  0.0 81.4 jit_solution(11688130217306888470)
XLA Ops:
  0.0 0.0 copy-start.1
  0.0 0.0 copy-start
  0.0 0.0 copy-start.2
  0.0 0.7 copy-done.1
  0.8 0.1 copy-done
  0.9 0.0 copy-done.2
  0.9 0.5 shard_map.38
  1.4 37.7 %all_to_all.10 = f32[128,1,768]{2,1,0:T(1,128)S(1)} all-to-all(f32[128,1,768]{2,1,0:T(1,128)S(1)} %bitcast.11), channel_id=1, replica_groups={{0,64,128,192,256,320,384,448,16,80,144,208,272,336,400,464,32,96,160,2..., dimensions={0} | all-to-all | bytes 786432 | tf_op jit(solution)/shard_map/all_to_all | solution.py:196
  39.1 3.1 %collective-permute-start = (f32[768,128]{1,0:T(8,128)S(1)}, f32[768,128]{1,0:T(8,128)S(1)}, u32[]{:S(2)}, u32[]{:S(2)}) collective-permute-start(f32[768,128]{1,0:T(8,128)S(1)} %bitcast.6), channel_id=1, source_target_pairs={{0,2},{1,3},{2,0},{3,1},{4,6},{5,7},{6,4},{7,5},{8,10},{9,11},{10,... | collective-permute-start | bytes 1179656 | tf_op jit(solution)/shard_map/ppermute | solution.py:201
  42.2 1.9 %collective-permute-start.1 = (f32[256,128]{1,0:T(8,128)S(1)}, f32[256,128]{1,0:T(8,128)S(1)}, u32[]{:S(2)}, u32[]{:S(2)}) collective-permute-start(f32[256,128]{1,0:T(8,128)S(1)} %shard_map.39), channel_id=1, source_target_pairs={{0,4},{4,0},{8,12},{12,8},{16,20},{20,16},{24,28},{28,24},{32,36},... | collective-permute-start | bytes 393224 | tf_op jit(solution)/shard_map/ppermute | solution.py:201
  44.2 0.1 shard_map.41.choose_ref
  44.3 5.0 %collective-permute-start.2 = (f32[768,128]{1,0:T(8,128)S(1)}, f32[768,128]{1,0:T(8,128)S(1)}, u32[]{:S(2)}, u32[]{:S(2)}) collective-permute-start(f32[768,128]{1,0:T(8,128)S(1)} %bitcast.8), channel_id=1, source_target_pairs={{0,1},{1,0},{2,3},{3,2},{4,5},{5,4},{6,7},{7,6},{8,9},{9,8},{10,11... | collective-permute-start | bytes 1179656 | tf_op jit(solution)/shard_map/ppermute | solution.py:201
  49.3 0.0 collective-permute-done.1.refs_0_
  49.3 1.1 %shard_map.40 = (bf16[512,512]{1,0:T(8,128)(2,1)S(1)}, f32[512,128]{1,0:T(8,128)S(1)}) custom-call(f32[256,128]{1,0:T(8,128)S(1)} %collective-permute-done.1.refs_0_, f32[768,128]{1,0:T(8,128)S(1)} %bitcast.9), custom_call_target="tpu_custom_call" | custom-call | flops 4096 | bytes 1024 | tf_op jit(solution)/shard_map/pallas_call | solution.py:184
  50.4 0.0 collective-permute-done.refs_2_
  50.4 4.6 %collective-permute-start.3 = (f32[768,128]{1,0:T(8,128)S(1)}, f32[768,128]{1,0:T(8,128)S(1)}, u32[]{:S(2)}, u32[]{:S(2)}) collective-permute-start(f32[768,128]{1,0:T(8,128)S(1)} %collective-permute-done.refs_2_), channel_id=1, source_target_pairs={{0,1},{1,0},{2,3},{3,2},{4,5},{5,4},{6,7},{7,6},{8,9},{9,8},{10,11... | collective-permute-start | bytes 1179656 | tf_op jit(solution)/shard_map/ppermute | solution.py:201
  55.0 0.9 %shard_map.42.refs_1_ = f32[512,128]{1,0:T(8,128)S(1)} custom-call(bf16[512,512]{1,0:T(8,128)(2,1)S(1)} %get-tuple-element.16.refs_0_, f32[512,128]{1,0:T(8,128)S(1)} %get-tuple-element.17.refs_1_, f32[768,128]{1,0:T(8,128)S(1)} %collective-permute-done.refs_2_), custom_call_target="tpu_custom_call" | custom-call | flops 4096 | bytes 1024 | tf_op jit(solution)/shard_map/pallas_call | solution.py:184
  55.9 0.0 collective-permute-done.2.refs_2_
  55.9 0.9 %shard_map.43.refs_1_ = f32[512,128]{1,0:T(8,128)S(1)} custom-call(bf16[512,512]{1,0:T(8,128)(2,1)S(1)} %get-tuple-element.16.refs_0_, f32[512,128]{1,0:T(8,128)S(1)} %shard_map.42.refs_1_, f32[768,128]{1,0:T(8,128)S(1)} %collective-permute-done.2.refs_2_), custom_call_target="tpu_custom_call" | custom-call | flops 4096 | bytes 1024 | tf_op jit(solution)/shard_map/pallas_call | solution.py:184
  56.8 0.0 collective-permute-done.3.refs_2_
  56.8 0.9 %shard_map.44 = f32[512,128]{1,0:T(8,128)S(1)} custom-call(bf16[512,512]{1,0:T(8,128)(2,1)S(1)} %get-tuple-element.16.refs_0_, f32[512,128]{1,0:T(8,128)S(1)} %shard_map.43.refs_1_, f32[768,128]{1,0:T(8,128)S(1)} %collective-permute-done.3.refs_2_), custom_call_target="tpu_custom_call" | custom-call | flops 4096 | bytes 1024 | tf_op jit(solution)/shard_map/pallas_call | solution.py:184
  57.7 22.8 %all_to_all.11 = f32[128,4,128]{2,1,0:T(4,128)S(1)} all-to-all(f32[128,4,128]{2,1,0:T(4,128)S(1)} %bitcast.10), channel_id=1, replica_groups={{0,64,128,192,256,320,384,448,16,80,144,208,272,336,400,464,32,96,160,2..., dimensions={0} | all-to-all | bytes 524288 | tf_op jit(solution)/shard_map/all_to_all | solution.py:196
  80.5 0.9 %shard_map.45 = f32[128,128]{1,0:T(8,128)} custom-call(bf16[128,512]{1,0:T(8,128)(2,1)S(1)} %shard_map.41.choose_ref, f32[512,128]{1,0:T(8,128)S(1)} %bitcast.12), custom_call_target="tpu_custom_call" | custom-call | flops 134217728 | bytes 1024 | tf_op jit(solution)/shard_map/pallas_call | solution.py:184
  (2 shorter events, 0.0 us)
Async XLA Ops:
  0.0 0.8 copy-start.1
  0.0 0.9 %copy-start = (f32[128,128]{1,0:T(8,128)S(1)}, f32[128,128]{1,0:T(8,128)}, u32[]{:S(2)}) copy-start(f32[128,128]{1,0:T(8,128)} %w_ref.1) | copy-start | bytes 196612
  0.0 0.8 %copy-start.2 = (s32[128,1]{0,1:T(1,128)S(1)}, s32[128,1]{0,1:T(1,128)}, u32[]{:S(2)}) copy-start(s32[128,1]{0,1:T(1,128)} %param.5) | copy-start | bytes 1540
  39.1 11.3 %collective-permute-start = (f32[768,128]{1,0:T(8,128)S(1)}, f32[768,128]{1,0:T(8,128)S(1)}, u32[]{:S(2)}, u32[]{:S(2)}) collective-permute-start(f32[768,128]{1,0:T(8,128)S(1)} %bitcast.6), channel_id=1, source_target_pairs={{0,2},{1,3},{2,0},{3,1},{4,6},{5,7},{6,4},{7,5},{8,10},{9,11},{10,... | collective-permute-start | bytes 1179656 | tf_op jit(solution)/shard_map/ppermute | solution.py:201
  42.2 7.1 %collective-permute-start.1 = (f32[256,128]{1,0:T(8,128)S(1)}, f32[256,128]{1,0:T(8,128)S(1)}, u32[]{:S(2)}, u32[]{:S(2)}) collective-permute-start(f32[256,128]{1,0:T(8,128)S(1)} %shard_map.39), channel_id=1, source_target_pairs={{0,4},{4,0},{8,12},{12,8},{16,20},{20,16},{24,28},{28,24},{32,36},... | collective-permute-start | bytes 393224 | tf_op jit(solution)/shard_map/ppermute | solution.py:201
  44.3 11.6 %collective-permute-start.2 = (f32[768,128]{1,0:T(8,128)S(1)}, f32[768,128]{1,0:T(8,128)S(1)}, u32[]{:S(2)}, u32[]{:S(2)}) collective-permute-start(f32[768,128]{1,0:T(8,128)S(1)} %bitcast.8), channel_id=1, source_target_pairs={{0,1},{1,0},{2,3},{3,2},{4,5},{5,4},{6,7},{7,6},{8,9},{9,8},{10,11... | collective-permute-start | bytes 1179656 | tf_op jit(solution)/shard_map/ppermute | solution.py:201
  50.4 6.4 %collective-permute-start.3 = (f32[768,128]{1,0:T(8,128)S(1)}, f32[768,128]{1,0:T(8,128)S(1)}, u32[]{:S(2)}, u32[]{:S(2)}) collective-permute-start(f32[768,128]{1,0:T(8,128)S(1)} %collective-permute-done.refs_2_), channel_id=1, source_target_pairs={{0,1},{1,0},{2,3},{3,2},{4,5},{5,4},{6,7},{7,6},{8,9},{9,8},{10,11... | collective-permute-start | bytes 1179656 | tf_op jit(solution)/shard_map/ppermute | solution.py:201

commit v4 on v3

--- a/solution.py
+++ b/solution.py
@@ -58,10 +58,11 @@
     out_ref[...] = mask_bf16(iota(out_ref.shape, 0) < iota(out_ref.shape, 1))
 
 
-def place(node):
+def place(node, odd):
     x = jnp.bitwise_and(node, NODE_X - 1)
     z = jnp.bitwise_and(node // NODE_X, NODE_Z - 1)
-    return (x * NODE_Z + z) * NODE_Y + node // (NODE_X * NODE_Z)
+    rank = (x * NODE_Z + z) * NODE_Y + node // (NODE_X * NODE_Z)
+    return jnp.where(odd, NODE_X * NODE_Y * NODE_Z - 1 - rank, rank)
 
 
 def pack_kernel(earlier_ref, leaf_ref, xt_ref, w_ref, out_ref, pos_ref):
@@ -72,8 +73,9 @@
     own = row == leaf
     before = nn(mask_bf16(own), earlier_ref[...])
     slot = jnp.sum(jnp.where(own, before, 0.0), axis=0, keepdims=True).astype(jnp.int32)
-    pos_ref[...] = place(leaf) * CAP + slot
-    goal = place(jnp.bitwise_xor(leaf, 1)) * CAP + slot
+    odd = lax.axis_index("slab") % 2 == 1
+    pos_ref[...] = place(leaf, odd) * CAP + slot
+    goal = place(jnp.bitwise_xor(leaf, 1), odd) * CAP + slot
     choose = [mask_bf16(row * CAP == goal - j) for j in range(CAP)]
     w_parts = jnp.concatenate(split3(w_ref[...]), axis=1)
     for j in range(CAP):
@@ -193,7 +195,11 @@
 
 def exchanged(value):
     order = [(y * NODE_Z + z) * NODE_X + x for x in range(NODE_X) for z in range(NODE_Z) for y in range(NODE_Y)]
-    return lax.all_to_all(value, "node", split_axis=0, concat_axis=0, axis_index_groups=[order], tiled=True)
+    n_slab = lax.axis_size("slab")
+    groups = [[n * n_slab + s for n in (order if s % 2 == 0 else order[::-1])] for s in range(n_slab)]
+    return lax.all_to_all(
+        value, ("node", "slab"), split_axis=0, concat_axis=0, axis_index_groups=groups, tiled=True
+    )
 
 
 def swapped(value, axis, mask):

time: 81.7 us -> 79.2 us (0.969)
  the two profiles are of different devices: /device:TPU:1 before, /device:TPU:8 now
where the time goes in v4:
time: 79.2 us; the launch traced here: 78.8 us
  blocking collectives  60.6 us (77%)
  starting transfers between devices  9.31 us (12%)
  Pallas kernels  5.22 us (7%)
  waiting for transfers between devices  2.71 us (3%)
  local copies, waits for them, and re-layouts  0.84 us (1%)
    all_to_all x2, blocking collectives, exchanged(): lax.all_to_all(value, ('node', 'slab'), split_axis=0, concat_axis=0, axis...  60.6 us
    ppermute x4, starting transfers between devices, swapped(): return lax.ppermute(value, axis, pairs)  9.31 us
    pallas_call x9, Pallas kernels, call(): pl.pallas_call(kernel, out_shape=outs[0] if single else outs, in_specs=wh...  5.22 us
    ppermute x4, waiting for transfers between devices, swapped(): return lax.ppermute(value, axis, pairs)  2.71 us
  transfers between devices with their start and end apart: 4, of which 1 were waited for; matrix products, arithmetic and copies ran while one was open for 0% of the time, Pallas kernels for 4%

profile of v4, /device:TPU:8, one launch (start us, length us, event | category | flops | bytes accessed | tf_op | source)
XLA Modules:
  0.0 78.8 jit_solution(17190533751676145818)
XLA Ops:
  0.0 0.0 copy-start.1
  0.0 0.0 copy-start
  0.0 0.0 copy-start.2
  0.0 0.7 copy-done.1
  0.8 0.1 copy-done
  0.9 0.0 copy-done.2
  0.9 0.5 shard_map.38
  1.4 35.6 %all_to_all.10 = f32[128,1,768]{2,1,0:T(1,128)S(1)} all-to-all(f32[128,1,768]{2,1,0:T(1,128)S(1)} %bitcast.11), channel_id=1, replica_groups={{0,64,128,192,256,320,384,448,16,80,144,208,272,336,400,464,32,96,160,2..., dimensions={0} | all-to-all | bytes 786432 | tf_op jit(solution)/shard_map/all_to_all | solution.py:200
  37.0 3.4 %collective-permute-start = (f32[768,128]{1,0:T(8,128)S(1)}, f32[768,128]{1,0:T(8,128)S(1)}, u32[]{:S(2)}, u32[]{:S(2)}) collective-permute-start(f32[768,128]{1,0:T(8,128)S(1)} %bitcast.6), channel_id=1, source_target_pairs={{0,2},{1,3},{2,0},{3,1},{4,6},{5,7},{6,4},{7,5},{8,10},{9,11},{10,... | collective-permute-start | bytes 1179656 | tf_op jit(solution)/shard_map/ppermute | solution.py:207
  40.4 2.1 %collective-permute-start.1 = (f32[256,128]{1,0:T(8,128)S(1)}, f32[256,128]{1,0:T(8,128)S(1)}, u32[]{:S(2)}, u32[]{:S(2)}) collective-permute-start(f32[256,128]{1,0:T(8,128)S(1)} %shard_map.39), channel_id=1, source_target_pairs={{0,4},{4,0},{8,12},{12,8},{16,20},{20,16},{24,28},{28,24},{32,36},... | collective-permute-start | bytes 393224 | tf_op jit(solution)/shard_map/ppermute | solution.py:207
  42.5 0.1 shard_map.41.choose_ref
  42.6 1.9 %collective-permute-start.2 = (f32[768,128]{1,0:T(8,128)S(1)}, f32[768,128]{1,0:T(8,128)S(1)}, u32[]{:S(2)}, u32[]{:S(2)}) collective-permute-start(f32[768,128]{1,0:T(8,128)S(1)} %bitcast.8), channel_id=1, source_target_pairs={{0,1},{1,0},{2,3},{3,2},{4,5},{5,4},{6,7},{7,6},{8,9},{9,8},{10,11... | collective-permute-start | bytes 1179656 | tf_op jit(solution)/shard_map/ppermute | solution.py:207
  44.5 2.7 %collective-permute-done.1.refs_0_ = f32[256,128]{1,0:T(8,128)S(1)} collective-permute-done((f32[256,128]{1,0:T(8,128)S(1)}, f32[256,128]{1,0:T(8,128)S(1)}, u32[]{:S(2)}, u32[]{:S(2)}) %collective-permute-start.1) | collective-permute-done | bytes 131104 | tf_op jit(solution)/shard_map/ppermute | solution.py:207
  47.2 1.1 %shard_map.40 = (bf16[512,512]{1,0:T(8,128)(2,1)S(1)}, f32[512,128]{1,0:T(8,128)S(1)}) custom-call(f32[256,128]{1,0:T(8,128)S(1)} %collective-permute-done.1.refs_0_, f32[768,128]{1,0:T(8,128)S(1)} %bitcast.9), custom_call_target="tpu_custom_call" | custom-call | flops 4096 | bytes 1024 | tf_op jit(solution)/shard_map/pallas_call | solution.py:186
  48.4 0.0 collective-permute-done.refs_2_
  48.4 1.9 %collective-permute-start.3 = (f32[768,128]{1,0:T(8,128)S(1)}, f32[768,128]{1,0:T(8,128)S(1)}, u32[]{:S(2)}, u32[]{:S(2)}) collective-permute-start(f32[768,128]{1,0:T(8,128)S(1)} %collective-permute-done.refs_2_), channel_id=1, source_target_pairs={{0,1},{1,0},{2,3},{3,2},{4,5},{5,4},{6,7},{7,6},{8,9},{9,8},{10,11... | collective-permute-start | bytes 1179656 | tf_op jit(solution)/shard_map/ppermute | solution.py:207
  50.3 0.9 %shard_map.42.refs_1_ = f32[512,128]{1,0:T(8,128)S(1)} custom-call(bf16[512,512]{1,0:T(8,128)(2,1)S(1)} %get-tuple-element.16.refs_0_, f32[512,128]{1,0:T(8,128)S(1)} %get-tuple-element.17.refs_1_, f32[768,128]{1,0:T(8,128)S(1)} %collective-permute-done.refs_2_), custom_call_target="tpu_custom_call" | custom-call | flops 4096 | bytes 1024 | tf_op jit(solution)/shard_map/pallas_call | solution.py:186
  51.2 0.0 collective-permute-done.2.refs_2_
  51.2 0.9 %shard_map.43.refs_1_ = f32[512,128]{1,0:T(8,128)S(1)} custom-call(bf16[512,512]{1,0:T(8,128)(2,1)S(1)} %get-tuple-element.16.refs_0_, f32[512,128]{1,0:T(8,128)S(1)} %shard_map.42.refs_1_, f32[768,128]{1,0:T(8,128)S(1)} %collective-permute-done.2.refs_2_), custom_call_target="tpu_custom_call" | custom-call | flops 4096 | bytes 1024 | tf_op jit(solution)/shard_map/pallas_call | solution.py:186
  52.1 0.0 collective-permute-done.3.refs_2_
  52.1 0.9 %shard_map.44 = f32[512,128]{1,0:T(8,128)S(1)} custom-call(bf16[512,512]{1,0:T(8,128)(2,1)S(1)} %get-tuple-element.16.refs_0_, f32[512,128]{1,0:T(8,128)S(1)} %shard_map.43.refs_1_, f32[768,128]{1,0:T(8,128)S(1)} %collective-permute-done.3.refs_2_), custom_call_target="tpu_custom_call" | custom-call | flops 4096 | bytes 1024 | tf_op jit(solution)/shard_map/pallas_call | solution.py:186
  52.9 25.0 %all_to_all.11 = f32[128,4,128]{2,1,0:T(4,128)S(1)} all-to-all(f32[128,4,128]{2,1,0:T(4,128)S(1)} %bitcast.10), channel_id=1, replica_groups={{0,64,128,192,256,320,384,448,16,80,144,208,272,336,400,464,32,96,160,2..., dimensions={0} | all-to-all | bytes 524288 | tf_op jit(solution)/shard_map/all_to_all | solution.py:200
  78.0 0.9 %shard_map.45 = f32[128,128]{1,0:T(8,128)} custom-call(bf16[128,512]{1,0:T(8,128)(2,1)S(1)} %shard_map.41.choose_ref, f32[512,128]{1,0:T(8,128)S(1)} %bitcast.12), custom_call_target="tpu_custom_call" | custom-call | flops 134217728 | bytes 1024 | tf_op jit(solution)/shard_map/pallas_call | solution.py:186
  (2 shorter events, 0.0 us)
Async XLA Ops:
  0.0 0.8 copy-start.1
  0.0 0.9 %copy-start = (f32[128,128]{1,0:T(8,128)S(1)}, f32[128,128]{1,0:T(8,128)}, u32[]{:S(2)}) copy-start(f32[128,128]{1,0:T(8,128)} %w_ref.1) | copy-start | bytes 196612
  0.0 0.8 %copy-start.2 = (s32[128,1]{0,1:T(1,128)S(1)}, s32[128,1]{0,1:T(1,128)}, u32[]{:S(2)}) copy-start(s32[128,1]{0,1:T(1,128)} %param.5) | copy-start | bytes 1540
  37.0 11.4 %collective-permute-start = (f32[768,128]{1,0:T(8,128)S(1)}, f32[768,128]{1,0:T(8,128)S(1)}, u32[]{:S(2)}, u32[]{:S(2)}) collective-permute-start(f32[768,128]{1,0:T(8,128)S(1)} %bitcast.6), channel_id=1, source_target_pairs={{0,2},{1,3},{2,0},{3,1},{4,6},{5,7},{6,4},{7,5},{8,10},{9,11},{10,... | collective-permute-start | bytes 1179656 | tf_op jit(solution)/shard_map/ppermute | solution.py:207
  40.4 6.9 %collective-permute-start.1 = (f32[256,128]{1,0:T(8,128)S(1)}, f32[256,128]{1,0:T(8,128)S(1)}, u32[]{:S(2)}, u32[]{:S(2)}) collective-permute-start(f32[256,128]{1,0:T(8,128)S(1)} %shard_map.39), channel_id=1, source_target_pairs={{0,4},{4,0},{8,12},{12,8},{16,20},{20,16},{24,28},{28,24},{32,36},... | collective-permute-start | bytes 393224 | tf_op jit(solution)/shard_map/ppermute | solution.py:207
  42.6 8.6 %collective-permute-start.2 = (f32[768,128]{1,0:T(8,128)S(1)}, f32[768,128]{1,0:T(8,128)S(1)}, u32[]{:S(2)}, u32[]{:S(2)}) collective-permute-start(f32[768,128]{1,0:T(8,128)S(1)} %bitcast.8), channel_id=1, source_target_pairs={{0,1},{1,0},{2,3},{3,2},{4,5},{5,4},{6,7},{7,6},{8,9},{9,8},{10,11... | collective-permute-start | bytes 1179656 | tf_op jit(solution)/shard_map/ppermute | solution.py:207
  48.4 3.7 %collective-permute-start.3 = (f32[768,128]{1,0:T(8,128)S(1)}, f32[768,128]{1,0:T(8,128)S(1)}, u32[]{:S(2)}, u32[]{:S(2)}) collective-permute-start(f32[768,128]{1,0:T(8,128)S(1)} %collective-permute-done.refs_2_), channel_id=1, source_target_pairs={{0,1},{1,0},{2,3},{3,2},{4,5},{5,4},{6,7},{7,6},{8,9},{9,8},{10,11... | collective-permute-start | bytes 1179656 | tf_op jit(solution)/shard_map/ppermute | solution.py:207

commit v5 on v3

--- a/solution.py
+++ b/solution.py
@@ -61,7 +61,8 @@
 def place(node):
     x = jnp.bitwise_and(node, NODE_X - 1)
     z = jnp.bitwise_and(node // NODE_X, NODE_Z - 1)
-    return (x * NODE_Z + z) * NODE_Y + node // (NODE_X * NODE_Z)
+    rank = (x * NODE_Z + z) * NODE_Y + node // (NODE_X * NODE_Z)
+    return NODE_X * NODE_Y * NODE_Z - 1 - rank
 
 
 def pack_kernel(earlier_ref, leaf_ref, xt_ref, w_ref, out_ref, pos_ref):
@@ -193,7 +194,7 @@
 
 def exchanged(value):
     order = [(y * NODE_Z + z) * NODE_X + x for x in range(NODE_X) for z in range(NODE_Z) for y in range(NODE_Y)]
-    return lax.all_to_all(value, "node", split_axis=0, concat_axis=0, axis_index_groups=[order], tiled=True)
+    return lax.all_to_all(value, "node", split_axis=0, concat_axis=0, axis_index_groups=[order[::-1]], tiled=True)
 
 
 def swapped(value, axis, mask):

time: 81.7 us -> 76 us (0.930)
  blocking collectives: 60.6 us -> 54.5 us
    all_to_all x2, blocking collectives: 60.6 us -> 54.5 us  [exchanged(): lax.all_to_all(value, 'node', split_axis=0, concat_axis=0, axis_index_gro...]
where the time goes in v5:
time: 76 us; the launch traced here: 75.1 us
  blocking collectives  54.5 us (72%)
  starting transfers between devices  14.5 us (19%)
  Pallas kernels  5.23 us (7%)
  local copies, waits for them, and re-layouts  0.84 us (1%)
    all_to_all x2, blocking collectives, exchanged(): lax.all_to_all(value, 'node', split_axis=0, concat_axis=0, axis_index_gro...  54.5 us
    ppermute x4, starting transfers between devices, swapped(): return lax.ppermute(value, axis, pairs)  14.5 us
    pallas_call x9, Pallas kernels, call(): pl.pallas_call(kernel, out_shape=outs[0] if single else outs, in_specs=wh...  5.23 us
  transfers between devices with their start and end apart: 4, of which 0 were waited for; matrix products, arithmetic and copies ran while one was open for 0% of the time, Pallas kernels for 4%

profile of v5, /device:TPU:1, one launch (start us, length us, event | category | flops | bytes accessed | tf_op | source)
XLA Modules:
  0.0 75.1 jit_solution(17112346131964664289)
XLA Ops:
  0.0 0.0 copy-start.1
  0.0 0.0 copy-start
  0.0 0.0 copy-start.2
  0.0 0.7 copy-done.1
  0.8 0.1 copy-done
  0.9 0.0 copy-done.2
  0.9 0.5 shard_map.38
  1.4 31.5 %all_to_all.10 = f32[128,1,768]{2,1,0:T(1,128)S(1)} all-to-all(f32[128,1,768]{2,1,0:T(1,128)S(1)} %bitcast.11), channel_id=1, replica_groups={{508,444,380,316,252,188,124,60,492,428,364,300,236,172,108,44,476,412,..., dimensions={0} | all-to-all | bytes 786432 | tf_op jit(solution)/shard_map/all_to_all | solution.py:197
  32.9 3.1 %collective-permute-start = (f32[768,128]{1,0:T(8,128)S(1)}, f32[768,128]{1,0:T(8,128)S(1)}, u32[]{:S(2)}, u32[]{:S(2)}) collective-permute-start(f32[768,128]{1,0:T(8,128)S(1)} %bitcast.6), channel_id=1, source_target_pairs={{0,2},{1,3},{2,0},{3,1},{4,6},{5,7},{6,4},{7,5},{8,10},{9,11},{10,... | collective-permute-start | bytes 1179656 | tf_op jit(solution)/shard_map/ppermute | solution.py:202
  36.0 2.4 %collective-permute-start.1 = (f32[256,128]{1,0:T(8,128)S(1)}, f32[256,128]{1,0:T(8,128)S(1)}, u32[]{:S(2)}, u32[]{:S(2)}) collective-permute-start(f32[256,128]{1,0:T(8,128)S(1)} %shard_map.39), channel_id=1, source_target_pairs={{0,4},{4,0},{8,12},{12,8},{16,20},{20,16},{24,28},{28,24},{32,36},... | collective-permute-start | bytes 393224 | tf_op jit(solution)/shard_map/ppermute | solution.py:202
  38.4 0.1 shard_map.41.choose_ref
  38.5 5.7 %collective-permute-start.2 = (f32[768,128]{1,0:T(8,128)S(1)}, f32[768,128]{1,0:T(8,128)S(1)}, u32[]{:S(2)}, u32[]{:S(2)}) collective-permute-start(f32[768,128]{1,0:T(8,128)S(1)} %bitcast.8), channel_id=1, source_target_pairs={{0,1},{1,0},{2,3},{3,2},{4,5},{5,4},{6,7},{7,6},{8,9},{9,8},{10,11... | collective-permute-start | bytes 1179656 | tf_op jit(solution)/shard_map/ppermute | solution.py:202
  44.2 0.0 collective-permute-done.1.refs_0_
  44.3 1.1 %shard_map.40 = (bf16[512,512]{1,0:T(8,128)(2,1)S(1)}, f32[512,128]{1,0:T(8,128)S(1)}) custom-call(f32[256,128]{1,0:T(8,128)S(1)} %collective-permute-done.1.refs_0_, f32[768,128]{1,0:T(8,128)S(1)} %bitcast.9), custom_call_target="tpu_custom_call" | custom-call | flops 4096 | bytes 1024 | tf_op jit(solution)/shard_map/pallas_call | solution.py:185
  45.4 0.0 collective-permute-done.refs_2_
  45.4 3.3 %collective-permute-start.3 = (f32[768,128]{1,0:T(8,128)S(1)}, f32[768,128]{1,0:T(8,128)S(1)}, u32[]{:S(2)}, u32[]{:S(2)}) collective-permute-start(f32[768,128]{1,0:T(8,128)S(1)} %collective-permute-done.refs_2_), channel_id=1, source_target_pairs={{0,1},{1,0},{2,3},{3,2},{4,5},{5,4},{6,7},{7,6},{8,9},{9,8},{10,11... | collective-permute-start | bytes 1179656 | tf_op jit(solution)/shard_map/ppermute | solution.py:202
  48.7 0.9 %shard_map.42.refs_1_ = f32[512,128]{1,0:T(8,128)S(1)} custom-call(bf16[512,512]{1,0:T(8,128)(2,1)S(1)} %get-tuple-element.16.refs_0_, f32[512,128]{1,0:T(8,128)S(1)} %get-tuple-element.17.refs_1_, f32[768,128]{1,0:T(8,128)S(1)} %collective-permute-done.refs_2_), custom_call_target="tpu_custom_call" | custom-call | flops 4096 | bytes 1024 | tf_op jit(solution)/shard_map/pallas_call | solution.py:185
  49.6 0.0 collective-permute-done.2.refs_2_
  49.6 0.9 %shard_map.43.refs_1_ = f32[512,128]{1,0:T(8,128)S(1)} custom-call(bf16[512,512]{1,0:T(8,128)(2,1)S(1)} %get-tuple-element.16.refs_0_, f32[512,128]{1,0:T(8,128)S(1)} %shard_map.42.refs_1_, f32[768,128]{1,0:T(8,128)S(1)} %collective-permute-done.2.refs_2_), custom_call_target="tpu_custom_call" | custom-call | flops 4096 | bytes 1024 | tf_op jit(solution)/shard_map/pallas_call | solution.py:185
  50.4 0.0 collective-permute-done.3.refs_2_
  50.5 0.9 %shard_map.44 = f32[512,128]{1,0:T(8,128)S(1)} custom-call(bf16[512,512]{1,0:T(8,128)(2,1)S(1)} %get-tuple-element.16.refs_0_, f32[512,128]{1,0:T(8,128)S(1)} %shard_map.43.refs_1_, f32[768,128]{1,0:T(8,128)S(1)} %collective-permute-done.3.refs_2_), custom_call_target="tpu_custom_call" | custom-call | flops 4096 | bytes 1024 | tf_op jit(solution)/shard_map/pallas_call | solution.py:185
  51.3 22.9 %all_to_all.11 = f32[128,4,128]{2,1,0:T(4,128)S(1)} all-to-all(f32[128,4,128]{2,1,0:T(4,128)S(1)} %bitcast.10), channel_id=1, replica_groups={{508,444,380,316,252,188,124,60,492,428,364,300,236,172,108,44,476,412,..., dimensions={0} | all-to-all | bytes 524288 | tf_op jit(solution)/shard_map/all_to_all | solution.py:197
  74.3 0.9 %shard_map.45 = f32[128,128]{1,0:T(8,128)} custom-call(bf16[128,512]{1,0:T(8,128)(2,1)S(1)} %shard_map.41.choose_ref, f32[512,128]{1,0:T(8,128)S(1)} %bitcast.12), custom_call_target="tpu_custom_call" | custom-call | flops 134217728 | bytes 1024 | tf_op jit(solution)/shard_map/pallas_call | solution.py:185
  (2 shorter events, 0.0 us)
Async XLA Ops:
  0.0 0.8 %copy-start.1 = (f32[128,64]{0,1:T(8,128)S(1)}, f32[128,64]{0,1:T(8,128)}, u32[]{:S(2)}) copy-start(f32[128,64]{0,1:T(8,128)} %param.3) | copy-start | bytes 98308
  0.0 0.9 %copy-start = (f32[128,128]{1,0:T(8,128)S(1)}, f32[128,128]{1,0:T(8,128)}, u32[]{:S(2)}) copy-start(f32[128,128]{1,0:T(8,128)} %w_ref.1) | copy-start | bytes 196612
  0.0 0.8 %copy-start.2 = (s32[128,1]{0,1:T(1,128)S(1)}, s32[128,1]{0,1:T(1,128)}, u32[]{:S(2)}) copy-start(s32[128,1]{0,1:T(1,128)} %param.5) | copy-start | bytes 1540
  32.9 12.5 %collective-permute-start = (f32[768,128]{1,0:T(8,128)S(1)}, f32[768,128]{1,0:T(8,128)S(1)}, u32[]{:S(2)}, u32[]{:S(2)}) collective-permute-start(f32[768,128]{1,0:T(8,128)S(1)} %bitcast.6), channel_id=1, source_target_pairs={{0,2},{1,3},{2,0},{3,1},{4,6},{5,7},{6,4},{7,5},{8,10},{9,11},{10,... | collective-permute-start | bytes 1179656 | tf_op jit(solution)/shard_map/ppermute | solution.py:202
  36.0 8.2 %collective-permute-start.1 = (f32[256,128]{1,0:T(8,128)S(1)}, f32[256,128]{1,0:T(8,128)S(1)}, u32[]{:S(2)}, u32[]{:S(2)}) collective-permute-start(f32[256,128]{1,0:T(8,128)S(1)} %shard_map.39), channel_id=1, source_target_pairs={{0,4},{4,0},{8,12},{12,8},{16,20},{20,16},{24,28},{28,24},{32,36},... | collective-permute-start | bytes 393224 | tf_op jit(solution)/shard_map/ppermute | solution.py:202
  38.5 11.0 %collective-permute-start.2 = (f32[768,128]{1,0:T(8,128)S(1)}, f32[768,128]{1,0:T(8,128)S(1)}, u32[]{:S(2)}, u32[]{:S(2)}) collective-permute-start(f32[768,128]{1,0:T(8,128)S(1)} %bitcast.8), channel_id=1, source_target_pairs={{0,1},{1,0},{2,3},{3,2},{4,5},{5,4},{6,7},{7,6},{8,9},{9,8},{10,11... | collective-permute-start | bytes 1179656 | tf_op jit(solution)/shard_map/ppermute | solution.py:202
  45.4 5.1 %collective-permute-start.3 = (f32[768,128]{1,0:T(8,128)S(1)}, f32[768,128]{1,0:T(8,128)S(1)}, u32[]{:S(2)}, u32[]{:S(2)}) collective-permute-start(f32[768,128]{1,0:T(8,128)S(1)} %collective-permute-done.refs_2_), channel_id=1, source_target_pairs={{0,1},{1,0},{2,3},{3,2},{4,5},{5,4},{6,7},{7,6},{8,9},{9,8},{10,11... | collective-permute-start | bytes 1179656 | tf_op jit(solution)/shard_map/ppermute | solution.py:202

commit v6 on v5

--- a/solution.py
+++ b/solution.py
@@ -61,7 +61,7 @@
 def place(node):
     x = jnp.bitwise_and(node, NODE_X - 1)
     z = jnp.bitwise_and(node // NODE_X, NODE_Z - 1)
-    rank = (x * NODE_Z + z) * NODE_Y + node // (NODE_X * NODE_Z)
+    rank = (z * NODE_X + jnp.bitwise_xor(x, x // 2)) * NODE_Y + node // (NODE_X * NODE_Z)
     return NODE_X * NODE_Y * NODE_Z - 1 - rank
 
 
@@ -76,23 +76,20 @@
     pos_ref[...] = place(leaf) * CAP + slot
     goal = place(jnp.bitwise_xor(leaf, 1)) * CAP + slot
     choose = [mask_bf16(row * CAP == goal - j) for j in range(CAP)]
-    w_parts = jnp.concatenate(split3(w_ref[...]), axis=1)
+    picked = nn(jnp.concatenate(choose, axis=0), jnp.concatenate(split3(w_ref[...]), axis=1))
+    picked = picked[:, :LANES] + picked[:, LANES : 2 * LANES] + picked[:, 2 * LANES :]
     for j in range(CAP):
-        picked = nn(choose[j], w_parts)
-        out_ref[pl.ds(j, LANES, stride=UNIT), :] = (
-            picked[:, :LANES] + picked[:, LANES : 2 * LANES] + picked[:, 2 * LANES :]
-        )
+        out_ref[pl.ds(j, LANES, stride=UNIT), :] = picked[j * LANES : (j + 1) * LANES, :]
     empty = jnp.zeros((dim, n), jnp.bfloat16)
     x_parts = []
     for part in split3(xt_ref[...]):
         x_parts.append(jnp.concatenate([part, empty], axis=1))
         x_parts.append(jnp.concatenate([empty, part], axis=1))
-    x_parts = jnp.concatenate(x_parts, axis=0)
+    pairs = [jnp.concatenate(choose[2 * h : 2 * h + 2], axis=1) for h in range(CAP // 2)]
+    picked = nt(jnp.concatenate(pairs, axis=0), jnp.concatenate(x_parts, axis=0))
+    picked = picked[:, :LANES] + picked[:, LANES : 2 * LANES] + picked[:, 2 * LANES :]
     for h in range(CAP // 2):
-        picked = nt(jnp.concatenate([choose[2 * h], choose[2 * h + 1]], axis=1), x_parts)
-        out_ref[pl.ds(CAP + h, LANES, stride=UNIT), :] = (
-            picked[:, :LANES] + picked[:, LANES : 2 * LANES] + picked[:, 2 * LANES :]
-        )
+        out_ref[pl.ds(CAP + h, LANES, stride=UNIT), :] = picked[h * LANES : (h + 1) * LANES, :]
 
 
 def doubled(pair):
@@ -129,19 +126,14 @@
     return jnp.concatenate(parts, axis=1)
 
 
-def block_kernel(*refs, first, last):
+def block_kernel(*refs, blocks, first, last):
     refs = list(refs)
     if first:
         own_ref = refs.pop(0)
     else:
         left_in, total_in = refs.pop(0), refs.pop(0)
-    cols_ref = refs.pop(0)
+    cols_refs, refs = refs[:blocks], refs[blocks:]
     rows = LANES
-    rights, values = [], []
-    for h in range(CAP // 2):
-        rights.append(right_operand(cols_ref[pl.ds(CAP + h, rows, stride=UNIT), :]))
-        w = jnp.concatenate([cols_ref[pl.ds(2 * h + e, rows, stride=UNIT), :] for e in range(2)], axis=0)
-        values.append(jnp.concatenate(split2(w), axis=1))
     if first:
         left_ref, total_ref = refs
         for h in range(CAP // 2):
@@ -152,10 +144,14 @@
         source = left_in
     left = source[...]
     main, rest = 0.0, 0.0
-    for h in range(CAP // 2):
-        w1, w2 = split2(jnp.exp2(nt(left, rights[h])))
-        main = main + nn(w1, values[h])
-        rest = rest + nn(w2, values[h][:, :LANES])
+    for cols_ref in cols_refs:
+        for h in range(CAP // 2):
+            right = right_operand(cols_ref[pl.ds(CAP + h, rows, stride=UNIT), :])
+            w = jnp.concatenate([cols_ref[pl.ds(2 * h + e, rows, stride=UNIT), :] for e in range(2)], axis=0)
+            high, low = split2(w)
+            w1, w2 = split2(jnp.exp2(nt(left, right)))
+            main = main + nn(w1, jnp.concatenate([high, low], axis=1))
+            rest = rest + nn(w2, high)
     total = main[:, :LANES] + (main[:, LANES:] + rest)
     if not first:
         total = total + total_in[...]
@@ -193,7 +189,8 @@
 
 
 def exchanged(value):
-    order = [(y * NODE_Z + z) * NODE_X + x for x in range(NODE_X) for z in range(NODE_Z) for y in range(NODE_Y)]
+    steps = [(z, k, y) for z in range(NODE_Z) for k in range(NODE_X) for y in range(NODE_Y)]
+    order = [(y * NODE_Z + z) * NODE_X + (k ^ (k // 2)) for z, k, y in steps]
     return lax.all_to_all(value, "node", split_axis=0, concat_axis=0, axis_index_groups=[order[::-1]], tiled=True)
 
 
@@ -223,19 +220,18 @@
     total_shape = jax.ShapeDtypeStruct((slots, LANES), f32)
     flops = 1 << 12
     left, total = call(
-        functools.partial(block_kernel, first=True, last=False),
+        functools.partial(block_kernel, blocks=1, first=True, last=False),
         (own, here),
         (jax.ShapeDtypeStruct((slots, 4 * LANES), jnp.bfloat16), total_shape),
         flops,
     )
-    middle = functools.partial(block_kernel, first=False, last=False)
+    middle = functools.partial(block_kernel, blocks=2, first=False, last=False)
     choose = call(choose_kernel, (pos,), (jax.ShapeDtypeStruct((leaf.shape[0], slots), bf16),), 1 << 12)
     far, total, choose = lax.optimization_barrier((far, total, choose))
     far_beside = swapped(far, "slab", 1)
-    total = call(middle, (left, total, far), (total_shape,), flops)
-    total = call(middle, (left, total, beside), (total_shape,), flops)
+    total = call(middle, (left, total, far, beside), (total_shape,), flops)
     total = call(
-        functools.partial(block_kernel, first=False, last=True), (left, total, far_beside), (total_shape,), flops
+        functools.partial(block_kernel, blocks=1, first=False, last=True), (left, total, far_beside), (total_shape,), flops
     )
     back = exchanged(total.reshape(n_node, CAP, LANES)).reshape(slots, LANES)
     return call(take_kernel, (choose, back), (jax.ShapeDtypeStruct(probes.shape, f32),), 1 << 27)

time: 76 us -> 75.4 us (level)
    pallas_call x9 -> x8, Pallas kernels: 5.23 us -> 5.12 us  [call(): pl.pallas_call(kernel, out_shape=outs[0] if single else outs, in_specs=wh...]
where the time goes in v6:
time: 75.4 us; the launch traced here: 75 us
  blocking collectives  54.6 us (72%)
  starting transfers between devices  14.3 us (19%)
  Pallas kernels  5.12 us (7%)
  local copies, waits for them, and re-layouts  0.84 us (1%)
    all_to_all x2, blocking collectives, exchanged(): lax.all_to_all(value, 'node', split_axis=0, concat_axis=0, axis_index_gro...  54.6 us
    ppermute x4, starting transfers between devices, swapped(): return lax.ppermute(value, axis, pairs)  14.3 us
    pallas_call x8, Pallas kernels, call(): pl.pallas_call(kernel, out_shape=outs[0] if single else outs, in_specs=wh...  5.12 us
  transfers between devices with their start and end apart: 4, of which 0 were waited for; matrix products, arithmetic and copies ran while one was open for 0% of the time, Pallas kernels for 4%

profile of v6, /device:TPU:1, one launch (start us, length us, event | category | flops | bytes accessed | tf_op | source)
XLA Modules:
  0.0 75.0 jit_solution(8157857450697797848)
XLA Ops:
  0.0 0.0 copy-start.1
  0.0 0.0 copy-start
  0.0 0.0 copy-start.2
  0.0 0.7 copy-done.1
  0.8 0.1 copy-done
  0.9 0.0 copy-done.2
  0.9 0.5 shard_map.38
  1.3 32.5 %all_to_all.10 = f32[128,1,768]{2,1,0:T(1,128)S(1)} all-to-all(f32[128,1,768]{2,1,0:T(1,128)S(1)} %bitcast.11), channel_id=1, replica_groups={{504,440,376,312,248,184,120,56,508,444,380,316,252,188,124,60,500,436,..., dimensions={0} | all-to-all | bytes 786432 | tf_op jit(solution)/shard_map/all_to_all | solution.py:194
  33.8 3.1 %collective-permute-start = (f32[768,128]{1,0:T(8,128)S(1)}, f32[768,128]{1,0:T(8,128)S(1)}, u32[]{:S(2)}, u32[]{:S(2)}) collective-permute-start(f32[768,128]{1,0:T(8,128)S(1)} %bitcast.6), channel_id=1, source_target_pairs={{0,2},{1,3},{2,0},{3,1},{4,6},{5,7},{6,4},{7,5},{8,10},{9,11},{10,... | collective-permute-start | bytes 1179656 | tf_op jit(solution)/shard_map/ppermute | solution.py:199
  36.9 1.9 %collective-permute-start.1 = (f32[256,128]{1,0:T(8,128)S(1)}, f32[256,128]{1,0:T(8,128)S(1)}, u32[]{:S(2)}, u32[]{:S(2)}) collective-permute-start(f32[256,128]{1,0:T(8,128)S(1)} %shard_map.39), channel_id=1, source_target_pairs={{0,4},{4,0},{8,12},{12,8},{16,20},{20,16},{24,28},{28,24},{32,36},... | collective-permute-start | bytes 393224 | tf_op jit(solution)/shard_map/ppermute | solution.py:199
  38.9 0.1 shard_map.41.choose_ref
  39.0 5.5 %collective-permute-start.2 = (f32[768,128]{1,0:T(8,128)S(1)}, f32[768,128]{1,0:T(8,128)S(1)}, u32[]{:S(2)}, u32[]{:S(2)}) collective-permute-start(f32[768,128]{1,0:T(8,128)S(1)} %bitcast.8), channel_id=1, source_target_pairs={{0,1},{1,0},{2,3},{3,2},{4,5},{5,4},{6,7},{7,6},{8,9},{9,8},{10,11... | collective-permute-start | bytes 1179656 | tf_op jit(solution)/shard_map/ppermute | solution.py:199
  44.5 0.0 collective-permute-done.1.refs_0_
  44.5 1.1 %shard_map.40 = (bf16[512,512]{1,0:T(8,128)(2,1)S(1)}, f32[512,128]{1,0:T(8,128)S(1)}) custom-call(f32[256,128]{1,0:T(8,128)S(1)} %collective-permute-done.1.refs_0_, f32[768,128]{1,0:T(8,128)S(1)} %bitcast.9), custom_call_target="tpu_custom_call" | custom-call | flops 4096 | bytes 1024 | tf_op jit(solution)/shard_map/pallas_call | solution.py:181
  45.6 0.0 collective-permute-done.refs_2_
  45.6 3.8 %collective-permute-start.3 = (f32[768,128]{1,0:T(8,128)S(1)}, f32[768,128]{1,0:T(8,128)S(1)}, u32[]{:S(2)}, u32[]{:S(2)}) collective-permute-start(f32[768,128]{1,0:T(8,128)S(1)} %collective-permute-done.refs_2_), channel_id=1, source_target_pairs={{0,1},{1,0},{2,3},{3,2},{4,5},{5,4},{6,7},{7,6},{8,9},{9,8},{10,11... | collective-permute-start | bytes 1179656 | tf_op jit(solution)/shard_map/ppermute | solution.py:199
  49.4 0.0 collective-permute-done.2.refs_3_
  49.4 1.7 %shard_map.42.refs_1_ = f32[512,128]{1,0:T(8,128)S(1)} custom-call(bf16[512,512]{1,0:T(8,128)(2,1)S(1)} %get-tuple-element.16.refs_0_, f32[512,128]{1,0:T(8,128)S(1)} %get-tuple-element.17.refs_1_, f32[768,128]{1,0:T(8,128)S(1)} %collective-permute-done.refs_2_, f32[768,128]{1,0:T(8,128)S(1)} %collective-permute-done.2.refs_3_), custom_call_target="tpu_custom_call" | custom-call | flops 4096 | bytes 1024 | tf_op jit(solution)/shard_map/pallas_call | solution.py:181
  51.1 0.0 collective-permute-done.3.refs_2_
  51.1 0.9 %shard_map.43 = f32[512,128]{1,0:T(8,128)S(1)} custom-call(bf16[512,512]{1,0:T(8,128)(2,1)S(1)} %get-tuple-element.16.refs_0_, f32[512,128]{1,0:T(8,128)S(1)} %shard_map.42.refs_1_, f32[768,128]{1,0:T(8,128)S(1)} %collective-permute-done.3.refs_2_), custom_call_target="tpu_custom_call" | custom-call | flops 4096 | bytes 1024 | tf_op jit(solution)/shard_map/pallas_call | solution.py:181
  52.0 22.2 %all_to_all.11 = f32[128,4,128]{2,1,0:T(4,128)S(1)} all-to-all(f32[128,4,128]{2,1,0:T(4,128)S(1)} %bitcast.10), channel_id=1, replica_groups={{504,440,376,312,248,184,120,56,508,444,380,316,252,188,124,60,500,436,..., dimensions={0} | all-to-all | bytes 524288 | tf_op jit(solution)/shard_map/all_to_all | solution.py:194
  74.2 0.9 %shard_map.44 = f32[128,128]{1,0:T(8,128)} custom-call(bf16[128,512]{1,0:T(8,128)(2,1)S(1)} %shard_map.41.choose_ref, f32[512,128]{1,0:T(8,128)S(1)} %bitcast.12), custom_call_target="tpu_custom_call" | custom-call | flops 134217728 | bytes 1024 | tf_op jit(solution)/shard_map/pallas_call | solution.py:181
  (2 shorter events, 0.0 us)
Async XLA Ops:
  0.0 0.8 %copy-start.1 = (f32[128,64]{0,1:T(8,128)S(1)}, f32[128,64]{0,1:T(8,128)}, u32[]{:S(2)}) copy-start(f32[128,64]{0,1:T(8,128)} %param.3) | copy-start | bytes 98308
  0.0 0.9 %copy-start = (f32[128,128]{1,0:T(8,128)S(1)}, f32[128,128]{1,0:T(8,128)}, u32[]{:S(2)}) copy-start(f32[128,128]{1,0:T(8,128)} %w_ref.1) | copy-start | bytes 196612
  0.0 0.8 %copy-start.2 = (s32[128,1]{0,1:T(1,128)S(1)}, s32[128,1]{0,1:T(1,128)}, u32[]{:S(2)}) copy-start(s32[128,1]{0,1:T(1,128)} %param.5) | copy-start | bytes 1540
  33.8 11.8 %collective-permute-start = (f32[768,128]{1,0:T(8,128)S(1)}, f32[768,128]{1,0:T(8,128)S(1)}, u32[]{:S(2)}, u32[]{:S(2)}) collective-permute-start(f32[768,128]{1,0:T(8,128)S(1)} %bitcast.6), channel_id=1, source_target_pairs={{0,2},{1,3},{2,0},{3,1},{4,6},{5,7},{6,4},{7,5},{8,10},{9,11},{10,... | collective-permute-start | bytes 1179656 | tf_op jit(solution)/shard_map/ppermute | solution.py:199
  36.9 7.6 %collective-permute-start.1 = (f32[256,128]{1,0:T(8,128)S(1)}, f32[256,128]{1,0:T(8,128)S(1)}, u32[]{:S(2)}, u32[]{:S(2)}) collective-permute-start(f32[256,128]{1,0:T(8,128)S(1)} %shard_map.39), channel_id=1, source_target_pairs={{0,4},{4,0},{8,12},{12,8},{16,20},{20,16},{24,28},{28,24},{32,36},... | collective-permute-start | bytes 393224 | tf_op jit(solution)/shard_map/ppermute | solution.py:199
  39.0 10.5 %collective-permute-start.2 = (f32[768,128]{1,0:T(8,128)S(1)}, f32[768,128]{1,0:T(8,128)S(1)}, u32[]{:S(2)}, u32[]{:S(2)}) collective-permute-start(f32[768,128]{1,0:T(8,128)S(1)} %bitcast.8), channel_id=1, source_target_pairs={{0,1},{1,0},{2,3},{3,2},{4,5},{5,4},{6,7},{7,6},{8,9},{9,8},{10,11... | collective-permute-start | bytes 1179656 | tf_op jit(solution)/shard_map/ppermute | solution.py:199
  45.6 5.5 %collective-permute-start.3 = (f32[768,128]{1,0:T(8,128)S(1)}, f32[768,128]{1,0:T(8,128)S(1)}, u32[]{:S(2)}, u32[]{:S(2)}) collective-permute-start(f32[768,128]{1,0:T(8,128)S(1)} %collective-permute-done.refs_2_), channel_id=1, source_target_pairs={{0,1},{1,0},{2,3},{3,2},{4,5},{5,4},{6,7},{7,6},{8,9},{9,8},{10,11... | collective-permute-start | bytes 1179656 | tf_op jit(solution)/shard_map/ppermute | solution.py:199

commit v7 on v6

--- a/solution.py
+++ b/solution.py
@@ -61,7 +61,11 @@
 def place(node):
     x = jnp.bitwise_and(node, NODE_X - 1)
     z = jnp.bitwise_and(node // NODE_X, NODE_Z - 1)
-    rank = (z * NODE_X + jnp.bitwise_xor(x, x // 2)) * NODE_Y + node // (NODE_X * NODE_Z)
+    y = node // (NODE_X * NODE_Z)
+    x = jnp.bitwise_xor(x, x // 2)
+    y = jnp.bitwise_xor(jnp.bitwise_xor(y, y // 2), y // 4)
+    z = jnp.bitwise_xor(z, z // 2)
+    rank = (z * NODE_Y + y) * NODE_X + x
     return NODE_X * NODE_Y * NODE_Z - 1 - rank
 
 
@@ -189,8 +193,8 @@
 
 
 def exchanged(value):
-    steps = [(z, k, y) for z in range(NODE_Z) for k in range(NODE_X) for y in range(NODE_Y)]
-    order = [(y * NODE_Z + z) * NODE_X + (k ^ (k // 2)) for z, k, y in steps]
+    gray = lambda count: [k ^ (k // 2) for k in range(count)]
+    order = [(y * NODE_Z + z) * NODE_X + x for z in gray(NODE_Z) for y in gray(NODE_Y) for x in gray(NODE_X)]
     return lax.all_to_all(value, "node", split_axis=0, concat_axis=0, axis_index_groups=[order[::-1]], tiled=True)
 
 

time: 75.4 us -> 74.5 us (0.988)
  starting transfers between devices: 14.3 us -> 13.4 us
    ppermute x4, starting transfers between devices: 14.3 us -> 13.4 us  [swapped(): return lax.ppermute(value, axis, pairs)]
  transfers between devices with their start and end apart: 4 -> 4, of which waited for: 0 -> 1; matrix products, arithmetic and copies ran while one was open for 0% -> 0% of each run, Pallas kernels for 4% -> 4%
where the time goes in v7:
time: 74.5 us; the launch traced here: 74.2 us
  blocking collectives  54.1 us (73%)
  starting transfers between devices  13.4 us (18%)
  Pallas kernels  5.12 us (7%)
  local copies, waits for them, and re-layouts  0.84 us (1%)
    all_to_all x2, blocking collectives, exchanged(): lax.all_to_all(value, 'node', split_axis=0, concat_axis=0, axis_index_gro...  54.1 us
    ppermute x4, starting transfers between devices, swapped(): return lax.ppermute(value, axis, pairs)  13.4 us
    pallas_call x8, Pallas kernels, call(): pl.pallas_call(kernel, out_shape=outs[0] if single else outs, in_specs=wh...  5.12 us
  transfers between devices with their start and end apart: 4, of which 1 were waited for; matrix products, arithmetic and copies ran while one was open for 0% of the time, Pallas kernels for 4%

profile of v7, /device:TPU:1, one launch (start us, length us, event | category | flops | bytes accessed | tf_op | source)
XLA Modules:
  0.0 74.2 jit_solution(9902153040225318703)
XLA Ops:
  0.0 0.0 copy-start.1
  0.0 0.0 copy-start
  0.0 0.0 copy-start.2
  0.0 0.7 copy-done.1
  0.8 0.1 copy-done
  0.9 0.0 copy-done.2
  0.9 0.5 shard_map.38
  1.3 32.0 %all_to_all.10 = f32[128,1,768]{2,1,0:T(1,128)S(1)} all-to-all(f32[128,1,768]{2,1,0:T(1,128)S(1)} %bitcast.11), channel_id=1, replica_groups={{296,300,292,288,360,364,356,352,488,492,484,480,424,428,420,416,168,17..., dimensions={0} | all-to-all | bytes 786432 | tf_op jit(solution)/shard_map/all_to_all | solution.py:198
  33.4 2.5 %collective-permute-start = (f32[768,128]{1,0:T(8,128)S(1)}, f32[768,128]{1,0:T(8,128)S(1)}, u32[]{:S(2)}, u32[]{:S(2)}) collective-permute-start(f32[768,128]{1,0:T(8,128)S(1)} %bitcast.6), channel_id=1, source_target_pairs={{0,2},{1,3},{2,0},{3,1},{4,6},{5,7},{6,4},{7,5},{8,10},{9,11},{10,... | collective-permute-start | bytes 1179656 | tf_op jit(solution)/shard_map/ppermute | solution.py:203
  35.8 2.2 %collective-permute-start.1 = (f32[256,128]{1,0:T(8,128)S(1)}, f32[256,128]{1,0:T(8,128)S(1)}, u32[]{:S(2)}, u32[]{:S(2)}) collective-permute-start(f32[256,128]{1,0:T(8,128)S(1)} %shard_map.39), channel_id=1, source_target_pairs={{0,4},{4,0},{8,12},{12,8},{16,20},{20,16},{24,28},{28,24},{32,36},... | collective-permute-start | bytes 393224 | tf_op jit(solution)/shard_map/ppermute | solution.py:203
  38.1 0.1 shard_map.41.choose_ref
  38.2 4.7 %collective-permute-start.2 = (f32[768,128]{1,0:T(8,128)S(1)}, f32[768,128]{1,0:T(8,128)S(1)}, u32[]{:S(2)}, u32[]{:S(2)}) collective-permute-start(f32[768,128]{1,0:T(8,128)S(1)} %bitcast.8), channel_id=1, source_target_pairs={{0,1},{1,0},{2,3},{3,2},{4,5},{5,4},{6,7},{7,6},{8,9},{9,8},{10,11... | collective-permute-start | bytes 1179656 | tf_op jit(solution)/shard_map/ppermute | solution.py:203
  43.0 0.0 collective-permute-done.1.refs_0_
  43.0 1.1 %shard_map.40 = (bf16[512,512]{1,0:T(8,128)(2,1)S(1)}, f32[512,128]{1,0:T(8,128)S(1)}) custom-call(f32[256,128]{1,0:T(8,128)S(1)} %collective-permute-done.1.refs_0_, f32[768,128]{1,0:T(8,128)S(1)} %bitcast.9), custom_call_target="tpu_custom_call" | custom-call | flops 4096 | bytes 1024 | tf_op jit(solution)/shard_map/pallas_call | solution.py:185
  44.1 0.6 collective-permute-done.refs_2_
  44.7 3.9 %collective-permute-start.3 = (f32[768,128]{1,0:T(8,128)S(1)}, f32[768,128]{1,0:T(8,128)S(1)}, u32[]{:S(2)}, u32[]{:S(2)}) collective-permute-start(f32[768,128]{1,0:T(8,128)S(1)} %collective-permute-done.refs_2_), channel_id=1, source_target_pairs={{0,1},{1,0},{2,3},{3,2},{4,5},{5,4},{6,7},{7,6},{8,9},{9,8},{10,11... | collective-permute-start | bytes 1179656 | tf_op jit(solution)/shard_map/ppermute | solution.py:203
  48.7 0.0 collective-permute-done.2.refs_3_
  48.7 1.7 %shard_map.42.refs_1_ = f32[512,128]{1,0:T(8,128)S(1)} custom-call(bf16[512,512]{1,0:T(8,128)(2,1)S(1)} %get-tuple-element.16.refs_0_, f32[512,128]{1,0:T(8,128)S(1)} %get-tuple-element.17.refs_1_, f32[768,128]{1,0:T(8,128)S(1)} %collective-permute-done.refs_2_, f32[768,128]{1,0:T(8,128)S(1)} %collective-permute-done.2.refs_3_), custom_call_target="tpu_custom_call" | custom-call | flops 4096 | bytes 1024 | tf_op jit(solution)/shard_map/pallas_call | solution.py:185
  50.4 0.0 collective-permute-done.3.refs_2_
  50.4 0.9 %shard_map.43 = f32[512,128]{1,0:T(8,128)S(1)} custom-call(bf16[512,512]{1,0:T(8,128)(2,1)S(1)} %get-tuple-element.16.refs_0_, f32[512,128]{1,0:T(8,128)S(1)} %shard_map.42.refs_1_, f32[768,128]{1,0:T(8,128)S(1)} %collective-permute-done.3.refs_2_), custom_call_target="tpu_custom_call" | custom-call | flops 4096 | bytes 1024 | tf_op jit(solution)/shard_map/pallas_call | solution.py:185
  51.2 22.1 %all_to_all.11 = f32[128,4,128]{2,1,0:T(4,128)S(1)} all-to-all(f32[128,4,128]{2,1,0:T(4,128)S(1)} %bitcast.10), channel_id=1, replica_groups={{296,300,292,288,360,364,356,352,488,492,484,480,424,428,420,416,168,17..., dimensions={0} | all-to-all | bytes 524288 | tf_op jit(solution)/shard_map/all_to_all | solution.py:198
  73.3 0.9 %shard_map.44 = f32[128,128]{1,0:T(8,128)} custom-call(bf16[128,512]{1,0:T(8,128)(2,1)S(1)} %shard_map.41.choose_ref, f32[512,128]{1,0:T(8,128)S(1)} %bitcast.12), custom_call_target="tpu_custom_call" | custom-call | flops 134217728 | bytes 1024 | tf_op jit(solution)/shard_map/pallas_call | solution.py:185
  (2 shorter events, 0.0 us)
Async XLA Ops:
  0.0 0.8 %copy-start.1 = (f32[128,64]{0,1:T(8,128)S(1)}, f32[128,64]{0,1:T(8,128)}, u32[]{:S(2)}) copy-start(f32[128,64]{0,1:T(8,128)} %param.3) | copy-start | bytes 98308
  0.0 0.9 %copy-start = (f32[128,128]{1,0:T(8,128)S(1)}, f32[128,128]{1,0:T(8,128)}, u32[]{:S(2)}) copy-start(f32[128,128]{1,0:T(8,128)} %w_ref.1) | copy-start | bytes 196612
  0.0 0.8 %copy-start.2 = (s32[128,1]{0,1:T(1,128)S(1)}, s32[128,1]{0,1:T(1,128)}, u32[]{:S(2)}) copy-start(s32[128,1]{0,1:T(1,128)} %param.5) | copy-start | bytes 1540
  33.4 11.4 %collective-permute-start = (f32[768,128]{1,0:T(8,128)S(1)}, f32[768,128]{1,0:T(8,128)S(1)}, u32[]{:S(2)}, u32[]{:S(2)}) collective-permute-start(f32[768,128]{1,0:T(8,128)S(1)} %bitcast.6), channel_id=1, source_target_pairs={{0,2},{1,3},{2,0},{3,1},{4,6},{5,7},{6,4},{7,5},{8,10},{9,11},{10,... | collective-permute-start | bytes 1179656 | tf_op jit(solution)/shard_map/ppermute | solution.py:203
  35.8 7.1 %collective-permute-start.1 = (f32[256,128]{1,0:T(8,128)S(1)}, f32[256,128]{1,0:T(8,128)S(1)}, u32[]{:S(2)}, u32[]{:S(2)}) collective-permute-start(f32[256,128]{1,0:T(8,128)S(1)} %shard_map.39), channel_id=1, source_target_pairs={{0,4},{4,0},{8,12},{12,8},{16,20},{20,16},{24,28},{28,24},{32,36},... | collective-permute-start | bytes 393224 | tf_op jit(solution)/shard_map/ppermute | solution.py:203
  38.2 10.5 %collective-permute-start.2 = (f32[768,128]{1,0:T(8,128)S(1)}, f32[768,128]{1,0:T(8,128)S(1)}, u32[]{:S(2)}, u32[]{:S(2)}) collective-permute-start(f32[768,128]{1,0:T(8,128)S(1)} %bitcast.8), channel_id=1, source_target_pairs={{0,1},{1,0},{2,3},{3,2},{4,5},{5,4},{6,7},{7,6},{8,9},{9,8},{10,11... | collective-permute-start | bytes 1179656 | tf_op jit(solution)/shard_map/ppermute | solution.py:203
  44.7 5.6 %collective-permute-start.3 = (f32[768,128]{1,0:T(8,128)S(1)}, f32[768,128]{1,0:T(8,128)S(1)}, u32[]{:S(2)}, u32[]{:S(2)}) collective-permute-start(f32[768,128]{1,0:T(8,128)S(1)} %collective-permute-done.refs_2_), channel_id=1, source_target_pairs={{0,1},{1,0},{2,3},{3,2},{4,5},{5,4},{6,7},{7,6},{8,9},{9,8},{10,11... | collective-permute-start | bytes 1179656 | tf_op jit(solution)/shard_map/ppermute | solution.py:203

commit v8 on v7

--- a/solution.py
+++ b/solution.py
@@ -64,8 +64,7 @@
     y = node // (NODE_X * NODE_Z)
     x = jnp.bitwise_xor(x, x // 2)
     y = jnp.bitwise_xor(jnp.bitwise_xor(y, y // 2), y // 4)
-    z = jnp.bitwise_xor(z, z // 2)
-    rank = (z * NODE_Y + y) * NODE_X + x
+    rank = (z * NODE_X + x) * NODE_Y + y
     return NODE_X * NODE_Y * NODE_Z - 1 - rank
 
 
@@ -194,7 +193,7 @@
 
 def exchanged(value):
     gray = lambda count: [k ^ (k // 2) for k in range(count)]
-    order = [(y * NODE_Z + z) * NODE_X + x for z in gray(NODE_Z) for y in gray(NODE_Y) for x in gray(NODE_X)]
+    order = [(y * NODE_Z + z) * NODE_X + x for z in range(NODE_Z) for x in gray(NODE_X) for y in gray(NODE_Y)]
     return lax.all_to_all(value, "node", split_axis=0, concat_axis=0, axis_index_groups=[order[::-1]], tiled=True)
 
 

time: 74.5 us -> 74.6 us (level)
  transfers between devices with their start and end apart: 4 -> 4, of which waited for: 1 -> 0; matrix products, arithmetic and copies ran while one was open for 0% -> 0% of each run, Pallas kernels for 4% -> 4%
where the time goes in v8:
time: 74.6 us; the launch traced here: 74.3 us
  blocking collectives  54.2 us (73%)
  starting transfers between devices  14 us (19%)
  Pallas kernels  5.12 us (7%)
  local copies, waits for them, and re-layouts  0.84 us (1%)
    all_to_all x2, blocking collectives, exchanged(): lax.all_to_all(value, 'node', split_axis=0, concat_axis=0, axis_index_gro...  54.2 us
    ppermute x4, starting transfers between devices, swapped(): return lax.ppermute(value, axis, pairs)  14 us
    pallas_call x8, Pallas kernels, call(): pl.pallas_call(kernel, out_shape=outs[0] if single else outs, in_specs=wh...  5.12 us
  transfers between devices with their start and end apart: 4, of which 0 were waited for; matrix products, arithmetic and copies ran while one was open for 0% of the time, Pallas kernels for 4%

profile of v8, /device:TPU:1, one launch (start us, length us, event | category | flops | bytes accessed | tf_op | source)
XLA Modules:
  0.0 74.3 jit_solution(8692544676736997278)
XLA Ops:
  0.0 0.0 copy-start.1
  0.0 0.0 copy-start
  0.0 0.0 copy-start.2
  0.0 0.7 copy-done.1
  0.8 0.1 copy-done
  0.9 0.0 copy-done.2
  0.9 0.5 shard_map.38
  1.3 32.3 %all_to_all.10 = f32[128,1,768]{2,1,0:T(1,128)S(1)} all-to-all(f32[128,1,768]{2,1,0:T(1,128)S(1)} %bitcast.11), channel_id=1, replica_groups={{312,376,504,440,184,248,120,56,316,380,508,444,188,252,124,60,308,372,..., dimensions={0} | all-to-all | bytes 786432 | tf_op jit(solution)/shard_map/all_to_all | solution.py:197
  33.6 3.1 %collective-permute-start = (f32[768,128]{1,0:T(8,128)S(1)}, f32[768,128]{1,0:T(8,128)S(1)}, u32[]{:S(2)}, u32[]{:S(2)}) collective-permute-start(f32[768,128]{1,0:T(8,128)S(1)} %bitcast.6), channel_id=1, source_target_pairs={{0,2},{1,3},{2,0},{3,1},{4,6},{5,7},{6,4},{7,5},{8,10},{9,11},{10,... | collective-permute-start | bytes 1179656 | tf_op jit(solution)/shard_map/ppermute | solution.py:202
  36.7 3.1 %collective-permute-start.1 = (f32[256,128]{1,0:T(8,128)S(1)}, f32[256,128]{1,0:T(8,128)S(1)}, u32[]{:S(2)}, u32[]{:S(2)}) collective-permute-start(f32[256,128]{1,0:T(8,128)S(1)} %shard_map.39), channel_id=1, source_target_pairs={{0,4},{4,0},{8,12},{12,8},{16,20},{20,16},{24,28},{28,24},{32,36},... | collective-permute-start | bytes 393224 | tf_op jit(solution)/shard_map/ppermute | solution.py:202
  39.8 0.1 shard_map.41.choose_ref
  39.9 3.9 %collective-permute-start.2 = (f32[768,128]{1,0:T(8,128)S(1)}, f32[768,128]{1,0:T(8,128)S(1)}, u32[]{:S(2)}, u32[]{:S(2)}) collective-permute-start(f32[768,128]{1,0:T(8,128)S(1)} %bitcast.8), channel_id=1, source_target_pairs={{0,1},{1,0},{2,3},{3,2},{4,5},{5,4},{6,7},{7,6},{8,9},{9,8},{10,11... | collective-permute-start | bytes 1179656 | tf_op jit(solution)/shard_map/ppermute | solution.py:202
  43.8 0.0 collective-permute-done.1.refs_0_
  43.8 1.1 %shard_map.40 = (bf16[512,512]{1,0:T(8,128)(2,1)S(1)}, f32[512,128]{1,0:T(8,128)S(1)}) custom-call(f32[256,128]{1,0:T(8,128)S(1)} %collective-permute-done.1.refs_0_, f32[768,128]{1,0:T(8,128)S(1)} %bitcast.9), custom_call_target="tpu_custom_call" | custom-call | flops 4096 | bytes 1024 | tf_op jit(solution)/shard_map/pallas_call | solution.py:184
  44.9 0.0 collective-permute-done.refs_2_
  44.9 4.0 %collective-permute-start.3 = (f32[768,128]{1,0:T(8,128)S(1)}, f32[768,128]{1,0:T(8,128)S(1)}, u32[]{:S(2)}, u32[]{:S(2)}) collective-permute-start(f32[768,128]{1,0:T(8,128)S(1)} %collective-permute-done.refs_2_), channel_id=1, source_target_pairs={{0,1},{1,0},{2,3},{3,2},{4,5},{5,4},{6,7},{7,6},{8,9},{9,8},{10,11... | collective-permute-start | bytes 1179656 | tf_op jit(solution)/shard_map/ppermute | solution.py:202
  48.9 0.0 collective-permute-done.2.refs_3_
  49.0 1.7 %shard_map.42.refs_1_ = f32[512,128]{1,0:T(8,128)S(1)} custom-call(bf16[512,512]{1,0:T(8,128)(2,1)S(1)} %get-tuple-element.16.refs_0_, f32[512,128]{1,0:T(8,128)S(1)} %get-tuple-element.17.refs_1_, f32[768,128]{1,0:T(8,128)S(1)} %collective-permute-done.refs_2_, f32[768,128]{1,0:T(8,128)S(1)} %collective-permute-done.2.refs_3_), custom_call_target="tpu_custom_call" | custom-call | flops 4096 | bytes 1024 | tf_op jit(solution)/shard_map/pallas_call | solution.py:184
  50.6 0.0 collective-permute-done.3.refs_2_
  50.7 0.9 %shard_map.43 = f32[512,128]{1,0:T(8,128)S(1)} custom-call(bf16[512,512]{1,0:T(8,128)(2,1)S(1)} %get-tuple-element.16.refs_0_, f32[512,128]{1,0:T(8,128)S(1)} %shard_map.42.refs_1_, f32[768,128]{1,0:T(8,128)S(1)} %collective-permute-done.3.refs_2_), custom_call_target="tpu_custom_call" | custom-call | flops 4096 | bytes 1024 | tf_op jit(solution)/shard_map/pallas_call | solution.py:184
  51.5 21.9 %all_to_all.11 = f32[128,4,128]{2,1,0:T(4,128)S(1)} all-to-all(f32[128,4,128]{2,1,0:T(4,128)S(1)} %bitcast.10), channel_id=1, replica_groups={{312,376,504,440,184,248,120,56,316,380,508,444,188,252,124,60,308,372,..., dimensions={0} | all-to-all | bytes 524288 | tf_op jit(solution)/shard_map/all_to_all | solution.py:197
  73.5 0.9 %shard_map.44 = f32[128,128]{1,0:T(8,128)} custom-call(bf16[128,512]{1,0:T(8,128)(2,1)S(1)} %shard_map.41.choose_ref, f32[512,128]{1,0:T(8,128)S(1)} %bitcast.12), custom_call_target="tpu_custom_call" | custom-call | flops 134217728 | bytes 1024 | tf_op jit(solution)/shard_map/pallas_call | solution.py:184
  (2 shorter events, 0.0 us)
Async XLA Ops:
  0.0 0.8 %copy-start.1 = (f32[128,64]{0,1:T(8,128)S(1)}, f32[128,64]{0,1:T(8,128)}, u32[]{:S(2)}) copy-start(f32[128,64]{0,1:T(8,128)} %param.3) | copy-start | bytes 98308
  0.0 0.9 %copy-start = (f32[128,128]{1,0:T(8,128)S(1)}, f32[128,128]{1,0:T(8,128)}, u32[]{:S(2)}) copy-start(f32[128,128]{1,0:T(8,128)} %w_ref.1) | copy-start | bytes 196612
  0.0 0.8 %copy-start.2 = (s32[128,1]{0,1:T(1,128)S(1)}, s32[128,1]{0,1:T(1,128)}, u32[]{:S(2)}) copy-start(s32[128,1]{0,1:T(1,128)} %param.5) | copy-start | bytes 1540
  33.6 11.3 %collective-permute-start = (f32[768,128]{1,0:T(8,128)S(1)}, f32[768,128]{1,0:T(8,128)S(1)}, u32[]{:S(2)}, u32[]{:S(2)}) collective-permute-start(f32[768,128]{1,0:T(8,128)S(1)} %bitcast.6), channel_id=1, source_target_pairs={{0,2},{1,3},{2,0},{3,1},{4,6},{5,7},{6,4},{7,5},{8,10},{9,11},{10,... | collective-permute-start | bytes 1179656 | tf_op jit(solution)/shard_map/ppermute | solution.py:202
  36.7 7.1 %collective-permute-start.1 = (f32[256,128]{1,0:T(8,128)S(1)}, f32[256,128]{1,0:T(8,128)S(1)}, u32[]{:S(2)}, u32[]{:S(2)}) collective-permute-start(f32[256,128]{1,0:T(8,128)S(1)} %shard_map.39), channel_id=1, source_target_pairs={{0,4},{4,0},{8,12},{12,8},{16,20},{20,16},{24,28},{28,24},{32,36},... | collective-permute-start | bytes 393224 | tf_op jit(solution)/shard_map/ppermute | solution.py:202
  39.9 9.0 %collective-permute-start.2 = (f32[768,128]{1,0:T(8,128)S(1)}, f32[768,128]{1,0:T(8,128)S(1)}, u32[]{:S(2)}, u32[]{:S(2)}) collective-permute-start(f32[768,128]{1,0:T(8,128)S(1)} %bitcast.8), channel_id=1, source_target_pairs={{0,1},{1,0},{2,3},{3,2},{4,5},{5,4},{6,7},{7,6},{8,9},{9,8},{10,11... | collective-permute-start | bytes 1179656 | tf_op jit(solution)/shard_map/ppermute | solution.py:202
  44.9 5.7 %collective-permute-start.3 = (f32[768,128]{1,0:T(8,128)S(1)}, f32[768,128]{1,0:T(8,128)S(1)}, u32[]{:S(2)}, u32[]{:S(2)}) collective-permute-start(f32[768,128]{1,0:T(8,128)S(1)} %collective-permute-done.refs_2_), channel_id=1, source_target_pairs={{0,1},{1,0},{2,3},{3,2},{4,5},{5,4},{6,7},{7,6},{8,9},{9,8},{10,11... | collective-permute-start | bytes 1179656 | tf_op jit(solution)/shard_map/ppermute | solution.py:202
